TPU v7x, 128 devices: a whole 4x4x4 slice. The times are simulated.
128 devices in a mesh: boxes: 128 (over y, z, x, core).
Axes of the slice: x: 4, y: 4, z: 4, core: 2. Of those that a mesh axis runs over, the one named last changes fastest.
Arguments:
- tile_mass: float32 [16384, 128], P('boxes'), may hold values from 0.5 to 2
- tile_frac: float32 [16384, 3, 128], P('boxes'), may hold values from 0 to 1
- tile_cell: int32 [16384, 128], P('boxes'), may hold values from 0 to 32767
- tile_level: int32 [16384, 128], P('boxes'), may hold values from 0 to 1
- tile_owner: int32 [16384, 1], P('boxes'), may hold values from 0 to 127; in each aligned block of 128 rows (0 to 127, 128 to 255, ...) at most 2 rows name the same one
- tile_count: int32 [128], P('boxes'), may hold values from 96 to 128, as said below
- box_owner: int32 [2, 128], replicated, may hold values from 0 to 127, each once within a row
- force_field: bfloat16 [2, 3, 4096, 1024], P(None, None, 'boxes'), may hold values from -6 to 6
Outputs:
- density: float32 [2, 4096, 1024], P(None, 'boxes')
- kick: float32 [16384, 3, 128], P('boxes')
Inputs may be any that keep to these rules, and one draw needn't show every extreme that they name: `tile_owner`: among the tiles of one device no owner is named by more than 2 tiles, a bound that some block reaches. The first tile_count tiles of a device are live, the rest are padding; some device has all 128 live. `box_owner`: each row is a permutation: every device holds exactly one box of each level. `tile_cell`: x * 32 * 32 + y * 32 + z for the cell (x, y, z) of the box.
All inputs are finite; a program needn't handle non-finite values.
Results may differ from a plain program's by a relative error of at most 0.0031.
Values may be sent and summed in bfloat16 or wider, within the bound.
A program may use at most 128 MiB of HBM per device.

v0:
```python
import functools

import jax
import jax.numpy as jnp
import numpy as np
from jax import lax
from jax.experimental import pallas as pl
from jax.experimental.pallas import tpu as pltpu
from jax.sharding import PartitionSpec as P

MESH = pl.DeviceIdType.MESH
HIGHEST = lax.Precision.HIGHEST
LAT_X = 4
LAT_Z = 4
SIDE = 32
CELLS = SIDE * SIDE
WIDE = CELLS + 128
INNER = 8
GROUP = 4

direction_table = np.array(
    [[1, 0, 0], [0, 1, 0], [0, 0, 1], [1, 1, 0], [1, 0, 1], [0, 1, 1], [1, 1, 1]], dtype=np.int32
)


def iota(shape, dim):
    return lax.broadcasted_iota(jnp.int32, shape, dim)


def rim_sources(box_owner):
    levels, devices = box_owner.shape
    lat_y = devices // 16
    places = jnp.arange(devices, dtype=jnp.int32)
    holder = jnp.sum(
        jnp.where(box_owner[:, None, :] == places[None, :, None], places[None, None, :], 0), axis=2
    )
    coords = jnp.stack([holder // (lat_y * LAT_Z), holder // LAT_Z % lat_y, holder % LAT_Z])
    extents = jnp.asarray([LAT_X, lat_y, LAT_Z], dtype=jnp.int32)[:, None, None, None]
    steps = jnp.asarray(direction_table.T)[:, None, :, None]
    ways = []
    for sign in (1, -1):
        near = (coords[:, :, None, :] + sign * steps + extents) % extents
        box = (near[0] * lat_y + near[1]) * LAT_Z + near[2]
        ways.append(
            jnp.sum(
                jnp.where(box[..., None] == places, box_owner[:, None, None, :], 0), axis=3
            ).reshape(levels * 7, devices)
        )
    return ways


def kind_of(lane):
    kind = jnp.where(lane < 32, 1, jnp.where(lane < 64, 2, -1))
    kind = jnp.where(lane == 64, 5, jnp.where(lane == 65, 3, kind))
    kind = jnp.where(lane == 66, 4, jnp.where(lane == 67, 6, kind))
    return jnp.where(lane >= 96, 0, kind)


def fold_target(lane):
    target = jnp.where(lane < CELLS, 96 + lane % SIDE, -1)
    target = jnp.where((lane >= CELLS) & (lane < CELLS + 32), 65, target)
    target = jnp.where((lane >= CELLS + 32) & (lane < CELLS + 64), 66, target)
    return jnp.where(lane == CELLS + 64, 67, target)


def fold_row(lane):
    row = jnp.where(lane < CELLS, lane // SIDE, -1)
    row = jnp.where((lane >= CELLS) & (lane < CELLS + 32), lane - CELLS, row)
    row = jnp.where((lane >= CELLS + 32) & (lane < CELLS + 64), lane - CELLS - 32, row)
    return jnp.where(lane == CELLS + 64, 0, row)


def fold(rows, dtype, precision):
    amount = rows.shape[0]
    shape = (SIDE, WIDE)
    own = fold_row(iota(shape, 1)) == iota(shape, 0)
    parts = [jnp.where(own, rows[place : place + 1, :], 0.0) for place in range(amount)]
    picked = jnp.concatenate(parts, axis=0).astype(dtype)
    target = fold_target(iota((WIDE, 128), 0)) == iota((WIDE, 128), 1)
    pick = jnp.where(target, 1.0, 0.0).astype(dtype)
    return jnp.dot(picked, pick, preferred_element_type=jnp.float32, precision=precision)


def unfold(table, dtype, precision):
    target = fold_target(iota((128, WIDE), 1)) == iota((128, WIDE), 0)
    pick = jnp.where(target, 1.0, 0.0).astype(dtype)
    spread = jnp.dot(table, pick, preferred_element_type=jnp.float32, precision=precision)
    shape = (SIDE, WIDE)
    own = fold_row(iota(shape, 1)) == iota(shape, 0)
    rows = []
    for place in range(table.shape[0] // SIDE):
        part = jnp.where(own, spread[place * SIDE : (place + 1) * SIDE, :], 0.0)
        rows.append(jnp.sum(part, axis=0, keepdims=True))
    return rows


def plane_pick(dtype, flip):
    shape = (128, CELLS) if flip else (CELLS, 128)
    lane = iota(shape, 0 if flip else 1)
    cell = iota(shape, 1 if flip else 0)
    wanted = jnp.where(lane < 32, lane, jnp.where(lane < 64, (lane - 32) * SIDE, -1))
    wanted = jnp.where(lane == 64, 0, wanted)
    return jnp.where(cell == wanted, 1.0, 0.0).astype(dtype)


def slot_picks(owner_ref, count, devices, by_slot):
    tiles = owner_ref.shape[1]
    across = jnp.broadcast_to(owner_ref[...], (tiles, tiles))
    down = jnp.transpose(across)
    same = across == down
    first, second = iota((tiles, tiles), 0), iota((tiles, tiles), 1)
    picks = []
    if by_slot:
        earlier = jnp.where(same & (first < second), 1.0, 0.0)
        rank = jnp.sum(earlier, axis=0, keepdims=True)
        fits = (across == first) & (second < count)
    else:
        earlier = jnp.where(same & (second < first), 1.0, 0.0)
        rank = jnp.sum(earlier, axis=1, keepdims=True)
        fits = (down == second) & (first < count)
    for order in range(2):
        picks.append(jnp.where(fits & (rank == float(order)), 1.0, 0.0))
    return picks


def greet(devices, me):
    barrier = pltpu.get_barrier_semaphore()

    def signal(step, carry):
        peer = lax.rem(me + step, devices)
        pl.semaphore_signal(barrier, inc=1, device_id=(peer,), device_id_type=MESH)
        return carry

    lax.fori_loop(1, devices, signal, 0)
    return barrier


def block_copy(source, target, send, recv, devices, me, step):
    peer = lax.rem(me + step, devices)
    return pltpu.make_async_remote_copy(
        src_ref=source.at[pl.ds(pl.multiple_of(peer * 8, 8), 8)],
        dst_ref=target.at[pl.ds(pl.multiple_of(me * 8, 8), 8)],
        send_sem=send.at[step - 1],
        recv_sem=recv.at[step - 1],
        device_id=(peer,),
        device_id_type=MESH,
    )


def inner_copy(gathered, send, recv, me, step):
    place = lax.rem(me, INNER)
    peer = me - place + lax.rem(place + step, INNER)
    return pltpu.make_async_remote_copy(
        src_ref=gathered.at[place],
        dst_ref=gathered.at[place],
        send_sem=send.at[step - 1],
        recv_sem=recv.at[step - 1],
        device_id=(peer,),
        device_id_type=MESH,
    )


def outer_copy(leaving, arrived, send, recv, devices, me, step):
    outer = devices // INNER
    row = me // INNER
    other = lax.rem(row + step, outer)
    return pltpu.make_async_remote_copy(
        src_ref=leaving.at[other],
        dst_ref=arrived.at[row],
        send_sem=send.at[step - 1],
        recv_sem=recv.at[step - 1],
        device_id=(other * INNER + lax.rem(me, INNER),),
        device_id_type=MESH,
    )


def each(count, act):
    def body(step, carry):
        act(step)
        return carry

    lax.fori_loop(1, count, body, 0)


def choose(tables, place_of, level, depth, dtype):
    lane = iota((1, 128), 1)
    kind = kind_of(lane)
    total = None
    for direction in range(7):
        keep = jnp.where(kind == direction, 1.0, 0.0).astype(dtype)
        block = tables[place_of(direction), level * depth : (level + 1) * depth, :]
        part = block * keep
        total = part if total is None else total + part
    return total


def relay(sources, gathered, leaving, arrived, devices, levels, depth, me, dtype):
    place, row = lax.rem(me, INNER), me // INNER

    def body(other, carry):
        target = other * INNER + place
        for level in range(levels):

            def place_of(direction):
                return lax.rem(sources[level * 7 + direction, target], INNER)

            leaving[other, level * depth : (level + 1) * depth, :] = choose(
                gathered, place_of, level, depth, dtype
            )
        return carry

    lax.fori_loop(0, devices // INNER, body, 0)
    arrived[row] = leaving[row]


def final_table(sources, arrived, level, depth, me, dtype):
    def row_of(direction):
        return sources[level * 7 + direction, me] // INNER

    return choose(arrived, row_of, level, depth, dtype)


def ship_kernel(
    devices,
    levels,
    sources,
    count_ref,
    owner_ref,
    mass_ref,
    frac_ref,
    cell_ref,
    level_ref,
    force_ref,
    inbox,
    rims,
    outbox,
    gathered,
    leaving,
    arrived,
    self_sem,
    tile_send,
    tile_recv,
    inner_send,
    inner_recv,
    outer_send,
    outer_recv,
):
    me = lax.axis_index("boxes")
    depth = 3 * SIDE
    bf16 = jnp.bfloat16
    barrier = greet(devices, me)
    force = force_ref[...]
    near = jnp.dot(force, plane_pick(bf16, False), preferred_element_type=jnp.float32)
    wide = []
    for place in range(levels * 3):
        at = place * SIDE
        front = force_ref[at : at + 16, :].astype(jnp.float32)[0:1, :]
        wide.append(jnp.concatenate([front, near[at : at + 1, :]], axis=1))
    table = near + fold(jnp.concatenate(wide, axis=0), bf16, None)
    gathered[lax.rem(me, INNER)] = table.astype(bf16)

    picks = slot_picks(owner_ref, count_ref[0], devices, True)
    cell = cell_ref[...]
    digits = [cell // CELLS, cell // SIDE % SIDE, cell % SIDE]
    fields = [jnp.where(level_ref[...] == 0, mass_ref[...], -mass_ref[...])]
    for axis in range(3):
        fields.append(digits[axis].astype(jnp.float32) + frac_ref[:, axis, :])
    for order in range(2):
        for place in range(4):
            moved = jnp.dot(
                picks[order], fields[place], preferred_element_type=jnp.float32, precision=HIGHEST
            )
            outbox[pl.ds(order * 4 + place, devices, stride=8), :] = moved

    pl.semaphore_wait(barrier, devices - 1)
    each(INNER, lambda step: inner_copy(gathered, inner_send, inner_recv, me, step).start())
    each(
        devices,
        lambda step: block_copy(outbox, inbox, tile_send, tile_recv, devices, me, step).start(),
    )
    own = pltpu.make_async_copy(
        outbox.at[pl.ds(pl.multiple_of(me * 8, 8), 8)],
        inbox.at[pl.ds(pl.multiple_of(me * 8, 8), 8)],
        self_sem,
    )
    own.start()
    each(INNER, lambda step: inner_copy(gathered, inner_send, inner_recv, me, step).wait())
    relay(sources, gathered, leaving, arrived, devices, levels, depth, me, bf16)
    outer = devices // INNER
    each(
        outer,
        lambda step: outer_copy(
            leaving, arrived, outer_send, outer_recv, devices, me, step
        ).start(),
    )
    each(
        outer,
        lambda step: outer_copy(leaving, arrived, outer_send, outer_recv, devices, me, step).wait(),
    )
    for level in range(levels):
        rims[level * depth : (level + 1) * depth, :] = final_table(
            sources, arrived, level, depth, me, bf16
        )
    own.wait()
    each(
        devices,
        lambda step: block_copy(outbox, inbox, tile_send, tile_recv, devices, me, step).wait(),
    )


def hat(coord, rows, start):
    ids = iota((rows, coord.shape[1]), 0).astype(jnp.float32) + start
    return jnp.maximum(0.0, 1.0 - jnp.abs(coord - ids))


def sweep_kernel(
    devices, levels, inbox, force_ref, rims, kicks, density, upper, table, cross, weighted, total
):
    bf16 = jnp.bfloat16
    rows = levels * 3 * SIDE
    depth = 3 * SIDE
    table[0:rows, 0:CELLS] = force_ref[...]
    table[0:rows, CELLS:WIDE] = rims[...]
    beyond = unfold(rims[...], bf16, None)
    beyond.append(jnp.zeros((16 - len(beyond), WIDE), jnp.float32))
    table[rows : rows + 16, :] = jnp.concatenate(beyond, axis=0).astype(bf16)
    cross[...] = jnp.zeros_like(cross)
    weighted[...] = jnp.zeros_like(weighted)
    total[...] = jnp.zeros_like(total)

    def advance(block, carry):
        info = []
        for part in range(GROUP):
            lanes = slice(part * 128, (part + 1) * 128)
            first = pl.multiple_of(block * (GROUP // 2 * 8), 8) + part * 4
            mass = inbox[pl.ds(first, 1), :]
            along = [inbox[pl.ds(first + 1 + axis, 1), :] for axis in range(3)]
            hat_x, hat_y, hat_z = [hat(along[axis], SIDE, 0.0) for axis in range(3)]
            end_x, end_y, end_z = [hat(along[axis], 1, float(SIDE)) for axis in range(3)]
            for y in range(SIDE):
                cross[y * SIDE : (y + 1) * SIDE, lanes] = (hat_y[y : y + 1, :] * hat_z).astype(bf16)
            cross[CELLS : CELLS + 32, lanes] = (end_y * hat_z).astype(bf16)
            cross[CELLS + 32 : CELLS + 64, lanes] = (hat_y * end_z).astype(bf16)
            last = jnp.where(iota((16, 128), 0) == 0, end_y * end_z, 0.0)
            cross[CELLS + 64 : CELLS + 80, lanes] = last.astype(bf16)
            for level in range(levels):
                own = jnp.maximum(mass if level == 0 else -mass, 0.0)
                weighted[level * SIDE : (level + 1) * SIDE, lanes] = (own * hat_x).astype(bf16)
            ends = jnp.where(iota((16, 128), 0) == 0, jnp.maximum(mass, 0.0), 0.0)
            ends = jnp.where(iota((16, 128), 0) == 1, jnp.maximum(-mass, 0.0), ends)
            weighted[2 * SIDE : 2 * SIDE + 16, lanes] = (ends * end_x).astype(bf16)
            info.append((first, mass, hat_x, end_x))
        total[...] += lax.dot_general(
            cross[...],
            weighted[...],
            (((1,), (1,)), ((), ())),
            preferred_element_type=jnp.float32,
        )
        sampled = jnp.dot(table[...], cross[...], preferred_element_type=jnp.float32)
        for part in range(GROUP):
            lanes = slice(part * 128, (part + 1) * 128)
            first, mass, hat_x, end_x = info[part]
            upper_level = mass < 0.0
            for axis in range(3):
                at = axis * SIDE
                picked = jnp.where(
                    upper_level,
                    sampled[depth + at : depth + at + SIDE, lanes],
                    sampled[at : at + SIDE, lanes],
                )
                far = jnp.where(
                    upper_level,
                    sampled[rows + 3 + axis : rows + 4 + axis, lanes],
                    sampled[rows + axis : rows + axis + 1, lanes],
                )
                value = jnp.sum(hat_x * picked, axis=0, keepdims=True) + end_x * far
                kicks[pl.ds(first + axis, 1), :] = value
            kicks[pl.ds(first + 3, 1), :] = jnp.zeros((1, 128), jnp.float32)
        return carry

    lax.fori_loop(0, 2 * devices // GROUP, advance, 0)
    flipped = jnp.transpose(total[...])
    density[...] = flipped[0 : levels * SIDE, 0:CELLS]
    wide = flipped[levels * SIDE : levels * SIDE + levels, :]
    upper[...] = jnp.where(
        iota((levels * SIDE, 128), 1) < 65, flipped[0 : levels * SIDE, CELLS:WIDE], 0.0
    ) + fold(wide, jnp.float32, HIGHEST)


def settle_kernel(
    devices,
    levels,
    sources,
    count_ref,
    owner_ref,
    kicks,
    density_in,
    upper,
    density,
    kick,
    returned,
    gathered,
    leaving,
    arrived,
    self_sem,
    tile_send,
    tile_recv,
    inner_send,
    inner_recv,
    outer_send,
    outer_recv,
):
    me = lax.axis_index("boxes")
    f32 = jnp.float32
    depth = SIDE
    barrier = greet(devices, me)
    gathered[lax.rem(me, INNER)] = upper[...]
    pl.semaphore_wait(barrier, devices - 1)
    each(INNER, lambda step: inner_copy(gathered, inner_send, inner_recv, me, step).start())
    each(
        devices,
        lambda step: block_copy(kicks, returned, tile_send, tile_recv, devices, me, step).start(),
    )
    own = pltpu.make_async_copy(
        kicks.at[pl.ds(pl.multiple_of(me * 8, 8), 8)],
        returned.at[pl.ds(pl.multiple_of(me * 8, 8), 8)],
        self_sem,
    )
    own.start()
    picks = slot_picks(owner_ref, count_ref[0], devices, False)
    each(INNER, lambda step: inner_copy(gathered, inner_send, inner_recv, me, step).wait())
    relay(sources, gathered, leaving, arrived, devices, levels, depth, me, f32)
    outer = devices // INNER
    each(
        outer,
        lambda step: outer_copy(
            leaving, arrived, outer_send, outer_recv, devices, me, step
        ).start(),
    )
    each(
        outer,
        lambda step: outer_copy(leaving, arrived, outer_send, outer_recv, devices, me, step).wait(),
    )
    table = jnp.concatenate(
        [final_table(sources, arrived, level, depth, me, f32) for level in range(levels)], axis=0
    )
    wide = unfold(table, f32, HIGHEST)
    first_row = iota((SIDE, 1), 0) == 0
    near = jnp.concatenate(
        [
            table[level * SIDE : (level + 1) * SIDE, :]
            + jnp.where(first_row, wide[level][:, CELLS:WIDE], 0.0)
            for level in range(levels)
        ],
        axis=0,
    )
    added = jnp.dot(near, plane_pick(f32, True), preferred_element_type=f32, precision=HIGHEST)
    for level in range(levels):
        at = slice(level * SIDE, (level + 1) * SIDE)
        density[at, :] = (
            density_in[at, :] + added[at, :] + jnp.where(first_row, wide[level][:, 0:CELLS], 0.0)
        )
    own.wait()
    each(
        devices,
        lambda step: block_copy(kicks, returned, tile_send, tile_recv, devices, me, step).wait(),
    )
    for axis in range(3):
        mine = None
        for order in range(2):
            part = jnp.dot(
                picks[order],
                returned[pl.ds(order * 4 + axis, devices, stride=8), :],
                preferred_element_type=f32,
                precision=HIGHEST,
            )
            mine = part if mine is None else mine + part
        kick[:, axis, :] = mine


def on_device(
    tile_mass, tile_frac, tile_cell, tile_level, tile_owner, tile_count, box_owner, force_field
):
    devices = lax.axis_size("boxes")
    levels = box_owner.shape[0]
    tiles, width = tile_mass.shape
    rows = levels * 3 * SIDE
    outer = devices // INNER
    f32, bf16 = jnp.float32, jnp.bfloat16
    shape = jax.ShapeDtypeStruct
    vmem = pl.BlockSpec(memory_space=pltpu.VMEM)
    smem = pl.BlockSpec(memory_space=pltpu.SMEM)
    hbm = pl.BlockSpec(memory_space=pl.ANY)
    dma = pltpu.SemaphoreType.DMA
    lower_from, upper_from = rim_sources(box_owner)
    owner_row = tile_owner.reshape(1, tiles)
    force = force_field.reshape(rows, CELLS)
    semaphores = [
        dma,
        dma((devices - 1,)),
        dma((devices - 1,)),
        dma((INNER - 1,)),
        dma((INNER - 1,)),
        dma((outer - 1,)),
        dma((outer - 1,)),
    ]
    inbox, rims = pl.pallas_call(
        functools.partial(ship_kernel, devices, levels),
        out_shape=(shape((devices * 8, width), f32), shape((rows, 128), bf16)),
        in_specs=[smem, smem] + [vmem] * 6,
        out_specs=(hbm, vmem),
        scratch_shapes=[
            pltpu.VMEM((devices * 8, width), f32),
            pltpu.VMEM((INNER, rows, 128), bf16),
            pltpu.VMEM((outer, rows, 128), bf16),
            pltpu.VMEM((outer, rows, 128), bf16),
        ]
        + semaphores,
        compiler_params=pltpu.CompilerParams(
            collective_id=0, has_side_effects=True, vmem_limit_bytes=40 << 20
        ),
        name="ship",
    )(lower_from, tile_count, owner_row, tile_mass, tile_frac, tile_cell, tile_level, force)
    kicks, density, upper = pl.pallas_call(
        functools.partial(sweep_kernel, devices, levels),
        out_shape=(
            shape((devices * 8, width), f32),
            shape((levels * SIDE, CELLS), f32),
            shape((levels * SIDE, 128), f32),
        ),
        in_specs=[vmem] * 3,
        out_specs=(vmem, vmem, vmem),
        scratch_shapes=[
            pltpu.VMEM((rows + 16, WIDE), bf16),
            pltpu.VMEM((WIDE, GROUP * 128), bf16),
            pltpu.VMEM((128, GROUP * 128), bf16),
            pltpu.VMEM((WIDE, 128), f32),
        ],
        compiler_params=pltpu.CompilerParams(vmem_limit_bytes=40 << 20),
        name="sweep",
    )(inbox, force, rims)
    density, kick = pl.pallas_call(
        functools.partial(settle_kernel, devices, levels),
        out_shape=(shape((levels * SIDE, CELLS), f32), shape((tiles, 3, width), f32)),
        in_specs=[smem, smem] + [vmem] * 4,
        out_specs=(vmem, vmem),
        scratch_shapes=[
            pltpu.VMEM((devices * 8, width), f32),
            pltpu.VMEM((INNER, levels * SIDE, 128), f32),
            pltpu.VMEM((outer, levels * SIDE, 128), f32),
            pltpu.VMEM((outer, levels * SIDE, 128), f32),
        ]
        + semaphores,
        compiler_params=pltpu.CompilerParams(
            collective_id=1, has_side_effects=True, vmem_limit_bytes=40 << 20
        ),
        name="settle",
    )(upper_from, tile_count, owner_row, kicks, density, upper)
    return (density.reshape(levels, SIDE, CELLS), kick)


def solution(mesh):
    in_specs = (
        P("boxes", None),
        P("boxes", None, None),
        P("boxes", None),
        P("boxes", None),
        P("boxes", None),
        P("boxes"),
        P(),
        P(None, None, "boxes", None),
    )
    out_specs = (P(None, "boxes", None), P("boxes", None, None))
    return jax.shard_map(
        on_device, mesh=mesh, in_specs=in_specs, out_specs=out_specs, check_vma=False
    )
```

profile of v0, /device:TPU:1, one launch (start us, length us, event | category | flops | bytes accessed | tf_op | source)
XLA Modules:
  0.0 129.7 jit_solution(13892138658196303367)
XLA Ops:
  0.6 0.0 copy-start.5
  0.6 0.0 copy-start.6
  0.7 0.0 copy-start
  1.4 0.8 select_reduce_fusion.2
  2.2 0.0 copy-done.5
  2.2 0.0 copy-done.6
  2.2 1.2 add_select_fusion.1
  3.5 1.8 %select_reduce_fusion = (s32[2,7,128]{2,1,0:T(8,128)S(1)}, s32[2,7,128]{2,1,0:T(8,128)S(1)}) fusion(s32[2,7,128]{2,1,0:T(8,128)S(1)} %get-tuple-element.30, s32[2,128]{1,0:T(2,128)} %param.18, s32[2,7,128]{2,1,0:T(8,128)S(1)} %get-tuple-element.31), kind=kLoop, calls=%fused_computation | loop fusion | flops 1372672 | bytes 29696 | tf_op jit(solution)/shard_map/reduce_sum | solution.py:45
  5.3 0.0 copy-start.1
  5.3 0.0 copy-start.2
  5.4 0.0 copy-start.3
  5.4 0.0 copy-start.4
  5.4 1.1 copy.16.frac_ref
  6.5 0.0 copy-done
  6.5 0.0 copy-done.1
  6.5 0.0 copy-done.2
  6.5 0.0 copy-done.3
  6.6 0.0 copy-done.4
  6.6 36.3 %ship.1 = (f32[1024,128]{1,0:T(8,128)S(1)}, bf16[192,128]{1,0:T(8,128)(2,1)S(1)}) custom-call(s32[14,128]{1,0:T(8,128)S(1)} %reshape.211.sources, s32[1]{0:T(128)S(6)} %copy.19.count_ref, s32[1,128]{1,0:T(1,128)S(1)} %bitcast.36, f32[128,128]{1,0:T(8,128)S(1)} %copy-done.1, f32[128,3,128]{2,1,0:T(4,128)S(1)} %copy.16.frac_ref, s32[128,128]{1,0:T(8,128)S(1)} %copy-done.2, ...), custom_call_target="tpu_custom_call" | custom-call | tf_op jit(solution)/shard_map/ship/pallas_call | solution.py:507
  42.9 52.6 %sweep.1 = (f32[1024,128]{1,0:T(8,128)S(1)}, f32[64,1024]{1,0:T(8,128)S(1)}, f32[64,128]{1,0:T(8,128)S(1)}) custom-call(f32[1024,128]{1,0:T(8,128)S(1)} %get-tuple-element.10.inbox, bf16[192,1024]{1,0:T(8,128)(2,1)S(1)} %bitcast.34, bf16[192,128]{1,0:T(8,128)(2,1)S(1)} %get-tuple-element.11.rims), custom_call_target="tpu_custom_call" | custom-call | tf_op jit(solution)/shard_map/sweep/pallas_call | solution.py:524
  95.5 32.8 %settle.1 = (f32[64,1024]{1,0:T(8,128)S(1)}, f32[128,3,128]{2,1,0:T(4,128)S(1)}) custom-call(s32[14,128]{1,0:T(8,128)S(1)} %reshape.209.sources, s32[1]{0:T(128)S(6)} %copy.19.count_ref, s32[1,128]{1,0:T(1,128)S(1)} %bitcast.37, f32[1024,128]{1,0:T(8,128)S(1)} %get-tuple-element.12.kicks, f32[64,1024]{1,0:T(8,128)S(1)} %get-tuple-element.13.density_in, ...), custom_call_target="tpu_custom_call" | custom-call | tf_op jit(solution)/shard_map/settle/pallas_call | solution.py:542
  128.3 0.7 copy.17
  129.0 0.7 copy.20
  (5 shorter events, 0.0 us)
Async XLA Ops:
  0.6 1.6 %copy-start.5 = (s32[3,7]{1,0:T(4,128)S(1)}, s32[3,7]{1,0:T(4,128)}, u32[]{:S(2)}) copy-start(s32[3,7]{1,0:T(4,128)} %constant.67) | copy-start | bytes 256
  0.6 1.6 %copy-start.6 = (s32[3,7]{1,0:T(4,128)S(1)}, s32[3,7]{1,0:T(4,128)}, u32[]{:S(2)}) copy-start(s32[3,7]{1,0:T(4,128)} %constant.64.clone) | copy-start | bytes 256
  0.7 5.9 %copy-start = (bf16[2,3,32,1024]{3,2,1,0:T(8,128)(2,1)S(1)}, bf16[2,3,32,1024]{3,2,1,0:T(8,128)(2,1)}, u32[]{:S(2)}) copy-start(bf16[2,3,32,1024]{3,2,1,0:T(8,128)(2,1)} %param.19) | copy-start | bytes 1179652
  5.3 1.2 copy-start.1
  5.3 1.2 copy-start.2
  5.4 1.2 copy-start.3
  5.4 1.2 copy-start.4
where the time goes:
time: 130 us
  Pallas kernels  122 us (94%)
  other arithmetic  3.89 us (3%)
  local copies, waits for them, and re-layouts  2.57 us (2%)
  between operations  1.52 us (1%)
    pallas_call x1, Pallas kernels, on_device(): pl.pallas_call(functools.partial(sweep_kernel, devices, levels), out_shap...  52.6 us
    pallas_call x1, Pallas kernels, on_device(): pl.pallas_call(functools.partial(ship_kernel, devices, levels), out_shape...  36.3 us
    pallas_call x1, Pallas kernels, on_device(): pl.pallas_call(functools.partial(settle_kernel, devices, levels), out_sha...  32.8 us

commit v1 on v0

v1 whole, which is shorter than its diff:
```python
import functools

import jax
import jax.numpy as jnp
import numpy as np
from jax import lax
from jax.experimental import pallas as pl
from jax.experimental.pallas import tpu as pltpu
from jax.sharding import PartitionSpec as P

MESH = pl.DeviceIdType.MESH
HIGHEST = lax.Precision.HIGHEST
F32 = jnp.float32
BF16 = jnp.bfloat16
LAT_X = 4
LAT_Z = 4
SIDE = 32
CELLS = SIDE * SIDE
WIDE = CELLS + 128
INNER = 8
SOURCES = 4
GROUP = 2 * SOURCES
LANES = GROUP * 128
CHUNK = 11
CHUNKS = 3
SHORT = (CHUNK + 1) * SIDE
RELAY_AT = 3

direction_table = np.array(
    [[1, 0, 0], [0, 1, 0], [0, 0, 1], [1, 1, 0], [1, 0, 1], [0, 1, 1], [1, 1, 1]], dtype=np.int32
)


def iota(shape, dim):
    return lax.broadcasted_iota(jnp.int32, shape, dim)


def ones_at(mask, dtype):
    return jnp.where(mask, 1.0, 0.0).astype(dtype)


def kind_of(lane):
    kind = jnp.where(lane < 32, 1, jnp.where(lane < 64, 2, -1))
    kind = jnp.where(lane == 64, 5, jnp.where(lane == 65, 3, kind))
    kind = jnp.where(lane == 66, 4, jnp.where(lane == 67, 6, kind))
    return jnp.where(lane >= 96, 0, kind)


def fold_target(lane):
    target = jnp.where(lane < CELLS, 96 + lane % SIDE, -1)
    target = jnp.where((lane >= CELLS) & (lane < CELLS + 32), 65, target)
    target = jnp.where((lane >= CELLS + 32) & (lane < CELLS + 64), 66, target)
    return jnp.where(lane == CELLS + 64, 67, target)


def fold_row(lane):
    row = jnp.where(lane < CELLS, lane // SIDE, -1)
    row = jnp.where((lane >= CELLS) & (lane < CELLS + 32), lane - CELLS, row)
    row = jnp.where((lane >= CELLS + 32) & (lane < CELLS + 64), lane - CELLS - 32, row)
    return jnp.where(lane == CELLS + 64, 0, row)


def fold(rows, dtype, precision):
    amount = rows.shape[0]
    shape = (SIDE, WIDE)
    own = fold_row(iota(shape, 1)) == iota(shape, 0)
    parts = [jnp.where(own, rows[place : place + 1, :], 0.0) for place in range(amount)]
    picked = jnp.concatenate(parts, axis=0).astype(dtype)
    pick = ones_at(fold_target(iota((WIDE, 128), 0)) == iota((WIDE, 128), 1), dtype)
    return jnp.dot(picked, pick, preferred_element_type=F32, precision=precision)


def unfold(table, dtype, precision):
    pick = ones_at(fold_target(iota((128, WIDE), 1)) == iota((128, WIDE), 0), dtype)
    spread = jnp.dot(table, pick, preferred_element_type=F32, precision=precision)
    shape = (SIDE, WIDE)
    own = fold_row(iota(shape, 1)) == iota(shape, 0)
    rows = []
    for place in range(table.shape[0] // SIDE):
        part = jnp.where(own, spread[place * SIDE : (place + 1) * SIDE, :], 0.0)
        rows.append(jnp.sum(part, axis=0, keepdims=True))
    return rows


def plane_pick(dtype, flip):
    shape = (128, CELLS) if flip else (CELLS, 128)
    lane = iota(shape, 0 if flip else 1)
    cell = iota(shape, 1 if flip else 0)
    wanted = jnp.where(lane < 32, lane, jnp.where(lane < 64, (lane - 32) * SIDE, -1))
    wanted = jnp.where(lane == 64, 0, wanted)
    return ones_at(cell == wanted, dtype)


def slot_picks(owner_ref, count, by_slot):
    tiles = owner_ref.shape[1]
    across = jnp.broadcast_to(owner_ref[...], (tiles, tiles))
    down = jnp.transpose(across)
    same = across == down
    first, second = iota((tiles, tiles), 0), iota((tiles, tiles), 1)
    if by_slot:
        earlier = jnp.where(same & (first < second), 1.0, 0.0)
        rank = jnp.sum(earlier, axis=0, keepdims=True)
        fits = (across == first) & (second < count)
    else:
        earlier = jnp.where(same & (second < first), 1.0, 0.0)
        rank = jnp.sum(earlier, axis=1, keepdims=True)
        fits = (down == second) & (first < count)
    picks = [jnp.where(fits & (rank == float(order)), 1.0, 0.0) for order in range(2)]
    return jnp.concatenate(picks, axis=0 if by_slot else 1)


def rim_sources(box_owner, level, devices):
    lat_y = devices // (LAT_X * LAT_Z)
    square = (devices, devices)
    across = jnp.broadcast_to(box_owner[level : level + 1, :], square)
    down = jnp.transpose(across).astype(F32).astype(BF16)
    hot = ones_at(across == iota(square, 0), BF16)
    places = iota(square, 0).astype(F32).astype(BF16)
    box = jnp.dot(hot, places, preferred_element_type=F32).astype(jnp.int32)
    at = [box // (lat_y * LAT_Z), box // LAT_Z % lat_y, box % LAT_Z]
    kind = kind_of(iota(square, 1))
    found = []
    for sign in (1, -1):
        hots = []
        for step in direction_table:
            near = [
                (at[axis] + (sign * int(step[axis]) + extent)) % extent
                for axis, extent in enumerate((LAT_X, lat_y, LAT_Z))
            ]
            wanted = (near[0] * lat_y + near[1]) * LAT_Z + near[2]
            hots.append(ones_at(wanted == iota(square, 1), BF16))
        owners = jnp.dot(jnp.concatenate(hots, axis=0), down, preferred_element_type=F32)
        total = jnp.zeros(square, F32)
        for direction in range(7):
            part = owners[direction * devices : (direction + 1) * devices, :]
            total = jnp.where(kind == direction, part, total)
        found.append(total)
    return found


def each(count, act):
    def body(step, carry):
        act(step)
        return carry

    lax.fori_loop(1, count, body, 0)


def block_rows(device):
    return pl.ds(pl.multiple_of(device * 8, 8), 8)


def block_copy(source, target, send, recv, devices, me, step):
    peer = lax.rem(me + step, devices)
    return pltpu.make_async_remote_copy(
        src_ref=source.at[block_rows(peer)],
        dst_ref=target.at[block_rows(me)],
        send_sem=send,
        recv_sem=recv,
        device_id=(peer,),
        device_id_type=MESH,
    )


def back_copy(source, target, send, recv, devices, me, step):
    peer = lax.rem(me + devices - step, devices)
    return pltpu.make_async_remote_copy(
        src_ref=source.at[block_rows(peer)],
        dst_ref=target.at[block_rows(me)],
        send_sem=send,
        recv_sem=recv,
        device_id=(peer,),
        device_id_type=MESH,
    )


def all_blocks(source, target, send, recv, devices, me):
    rows = (devices - 1) * 8
    return pltpu.make_async_remote_copy(
        src_ref=source.at[pl.ds(0, rows)],
        dst_ref=target.at[pl.ds(0, rows)],
        send_sem=send,
        recv_sem=recv,
        device_id=(lax.rem(me + 1, devices),),
        device_id_type=MESH,
    )


def inner_copy(gathered, send, recv, me, step):
    place = lax.rem(me, INNER)
    peer = me - place + lax.rem(place + step, INNER)
    return pltpu.make_async_remote_copy(
        src_ref=gathered.at[place],
        dst_ref=gathered.at[place],
        send_sem=send.at[step - 1],
        recv_sem=recv.at[step - 1],
        device_id=(peer,),
        device_id_type=MESH,
    )


def outer_copy(leaving, arrived, send, recv, devices, me, step):
    outer = devices // INNER
    row = me // INNER
    other = lax.rem(row + step, outer)
    return pltpu.make_async_remote_copy(
        src_ref=leaving.at[other],
        dst_ref=arrived.at[row],
        send_sem=send.at[step - 1],
        recv_sem=recv.at[step - 1],
        device_id=(other * INNER + lax.rem(me, INNER),),
        device_id_type=MESH,
    )


def choose(tables, wanted, level, depth, dtype):
    total = None
    for place in range(tables.shape[0]):
        keep = ones_at(wanted == float(place), dtype)
        part = tables[place, level * depth : (level + 1) * depth, :] * keep
        total = part if total is None else total + part
    return total


def relay(near, first, gathered, leaving, arrived, outer, levels, depth, me, dtype):
    place, row = lax.rem(me, INNER), me // INNER

    def body(other, carry):
        for level in range(levels):
            wanted = near[first + level, pl.ds(other * INNER + place, 1), :]
            wanted = wanted - INNER * jnp.floor(wanted / INNER)
            leaving[other, level * depth : (level + 1) * depth, :] = choose(
                gathered, wanted, level, depth, dtype
            )
        return carry

    lax.fori_loop(0, outer, body, 0)
    arrived[row] = leaving[row]


def final_table(near, first, arrived, level, depth, me, dtype):
    wanted = jnp.floor(near[first + level, pl.ds(me, 1), :] / INNER)
    return choose(arrived, wanted, level, depth, dtype)


def hat(coord, rows, start):
    ids = iota((rows, coord.shape[1]), 0).astype(F32) + start
    return jnp.maximum(0.0, 1.0 - jnp.abs(coord - ids))


def group_sources(devices, me, block):
    return [lax.rem(me + devices - (block * SOURCES + 1 + part), devices) for part in range(SOURCES)]


def group_fields(inbox, sources):
    fields = []
    for field in range(4):
        rows = []
        for source in sources:
            for order in range(2):
                rows.append(inbox[pl.ds(source * 8 + (order * 4 + field), 1), :])
        fields.append(jnp.concatenate(rows, axis=1))
    return fields


def fill_deposit(fields, short, weighted):
    mass, x, y, z = fields
    chunk = jnp.where(y >= 2.0 * CHUNK, 2.0, jnp.where(y >= CHUNK, 1.0, 0.0))
    hat_y = hat(y - chunk * CHUNK, 16, 0.0)
    hat_z = hat(z, SIDE, 0.0)
    for row in range(CHUNK + 1):
        short[row * SIDE : (row + 1) * SIDE, :] = (hat_y[row : row + 1, :] * hat_z).astype(BF16)
    tops = jnp.where(iota((16, LANES), 0) <= CHUNK, hat_y * hat(z, 1, float(SIDE)), 0.0)
    short[SHORT : SHORT + 16, :] = tops.astype(BF16)
    hat_x = hat(x, SIDE, 0.0)
    for place in range(CHUNKS):
        for level in range(2):
            own = jnp.maximum(mass if level == 0 else -mass, 0.0)
            own = jnp.where(chunk == float(place), own, 0.0)
            at = (place * 2 + level) * SIDE
            weighted[at : at + SIDE, :] = (own * hat_x).astype(BF16)
    row_of = 2.0 * chunk + jnp.where(mass < 0.0, 1.0, 0.0)
    ends = jnp.where(iota((16, LANES), 0).astype(F32) == row_of, jnp.abs(mass), 0.0)
    at = CHUNKS * 2 * SIDE
    weighted[at : at + 16, :] = (ends * hat(x, 1, float(SIDE))).astype(BF16)


def add_deposit(short, weighted, total):
    product = lax.dot_general(
        short[...], weighted[...], (((1,), (1,)), ((), ())), preferred_element_type=F32
    )
    total[:, 0 : product.shape[1]] += product


def fill_cross(fields, cross):
    _, _, y, z = fields
    hat_y, hat_z = hat(y, SIDE, 0.0), hat(z, SIDE, 0.0)
    end_y, end_z = hat(y, 1, float(SIDE)), hat(z, 1, float(SIDE))
    for row in range(SIDE):
        cross[row * SIDE : (row + 1) * SIDE, :] = (hat_y[row : row + 1, :] * hat_z).astype(BF16)
    cross[CELLS : CELLS + 32, :] = (end_y * hat_z).astype(BF16)
    cross[CELLS + 32 : CELLS + 64, :] = (hat_y * end_z).astype(BF16)
    last = jnp.where(iota((16, LANES), 0) == 0, end_y * end_z, 0.0)
    cross[CELLS + 64 : CELLS + 80, :] = last.astype(BF16)


def sample(fields, sources, table, cross, kicks):
    mass, x, _, _ = fields
    rows = table.shape[0] - 16
    depth = rows // 2
    sampled = jnp.dot(table[...], cross[...], preferred_element_type=F32)
    hat_x, end_x = hat(x, SIDE, 0.0), hat(x, 1, float(SIDE))
    upper_level = mass < 0.0
    for axis in range(3):
        at = axis * SIDE
        picked = jnp.where(
            upper_level, sampled[depth + at : depth + at + SIDE, :], sampled[at : at + SIDE, :]
        )
        at = rows + axis
        far = jnp.where(upper_level, sampled[at + 3 : at + 4, :], sampled[at : at + 1, :])
        value = jnp.sum(hat_x * picked, axis=0, keepdims=True) + end_x * far
        for part, source in enumerate(sources):
            for order in range(2):
                lanes = slice((part * 2 + order) * 128, (part * 2 + order + 1) * 128)
                kicks[pl.ds(source * 8 + (order * 4 + axis), 1), :] = value[:, lanes]


def spread_deposit(total, wide):
    wide[...] = jnp.zeros_like(wide)
    first, second = total[:, 0:128], total[:, 128:256]
    low = iota(first.shape, 1) < 2 * SIDE
    for place in range(CHUNKS):
        main = [first, pltpu.roll(first, 64, 1), second][place]
        ends = second if place == 0 else pltpu.roll(second, 128 - 2 * place, 1)
        both = jnp.where(low, main, ends)
        at = place * CHUNK * SIDE
        wide[at : at + SHORT, :] += both[0:SHORT, :]
        at = CELLS + SIDE + place * CHUNK
        wide[at : at + CHUNK + 1, :] += both[SHORT : SHORT + CHUNK + 1, :]


def kernel(
    devices,
    levels,
    count_ref,
    owner_ref,
    box_owner,
    mass_ref,
    frac_ref,
    cell_ref,
    level_ref,
    force_ref,
    density,
    kick,
    outbox,
    inbox,
    kicks,
    returned,
    near,
    force_gathered,
    force_leaving,
    force_arrived,
    mass_gathered,
    mass_leaving,
    mass_arrived,
    table,
    cross_a,
    cross_b,
    short_a,
    short_b,
    weighted_a,
    weighted_b,
    total,
    wide,
    own_sem,
    tile_send,
    tile_recv,
    kick_send,
    kick_recv,
    inner_send,
    inner_recv,
    outer_send,
    outer_recv,
    inner_send2,
    inner_recv2,
    outer_send2,
    outer_recv2,
):
    me = lax.axis_index("boxes")
    outer = devices // INNER
    depth = 3 * SIDE
    rows = levels * depth
    groups = devices // SOURCES
    pairs = groups // 2

    barrier = pltpu.get_barrier_semaphore()
    each(
        devices,
        lambda step: pl.semaphore_signal(
            barrier, inc=1, device_id=(lax.rem(me + step, devices),), device_id_type=MESH
        ),
    )

    picks = slot_picks(owner_ref, count_ref[0], True)
    cell = cell_ref[...]
    digits = [cell // CELLS, cell // SIDE % SIDE, cell % SIDE]
    fields = [jnp.where(level_ref[...] == 0, mass_ref[...], -mass_ref[...])]
    for axis in range(3):
        fields.append(digits[axis].astype(F32) + frac_ref[axis])
    packed = jnp.dot(
        picks, jnp.concatenate(fields, axis=1), preferred_element_type=F32, precision=HIGHEST
    )
    for order in range(2):
        for field in range(4):
            part = packed[order * devices : (order + 1) * devices, field * 128 : field * 128 + 128]
            outbox[pl.ds(order * 4 + field, devices, stride=8), :] = part

    force = force_ref[...]
    planes = jnp.dot(force, plane_pick(BF16, False), preferred_element_type=F32)
    fronts = []
    for place in range(levels * 3):
        at = place * SIDE
        front = force_ref[at : at + 16, :].astype(F32)[0:1, :]
        fronts.append(jnp.concatenate([front, planes[at : at + 1, :]], axis=1))
    lower = planes + fold(jnp.concatenate(fronts, axis=0), BF16, None)
    force_gathered[lax.rem(me, INNER)] = lower.astype(BF16)

    pl.semaphore_wait(barrier, devices - 1)
    each(
        INNER, lambda step: inner_copy(force_gathered, inner_send, inner_recv, me, step).start()
    )

    def tile_copy(step):
        return block_copy(outbox, inbox, tile_send, tile_recv.at[step - 1], devices, me, step)

    each(devices, lambda step: tile_copy(step).start())
    own = pltpu.make_async_copy(outbox.at[block_rows(me)], inbox.at[block_rows(me)], own_sem)
    own.start()

    for level in range(levels):
        forward, backward = rim_sources(box_owner, level, devices)
        near[level] = forward
        near[levels + level] = backward
    table[0:rows, 0:CELLS] = force
    cross_a[...] = jnp.zeros_like(cross_a)
    cross_b[...] = jnp.zeros_like(cross_b)
    total[...] = jnp.zeros_like(total)
    kicks[...] = jnp.zeros_like(kicks)

    def force_relay():
        each(
            INNER, lambda step: inner_copy(force_gathered, inner_send, inner_recv, me, step).wait()
        )
        relay(
            near, 0, force_gathered, force_leaving, force_arrived, outer, levels, depth, me, BF16
        )
        each(
            outer,
            lambda step: outer_copy(
                force_leaving, force_arrived, outer_send, outer_recv, devices, me, step
            ).start(),
        )

    def mass_relay():
        each(
            INNER,
            lambda step: inner_copy(mass_gathered, inner_send2, inner_recv2, me, step).wait(),
        )
        relay(
            near, levels, mass_gathered, mass_leaving, mass_arrived, outer, levels, SIDE, me, F32
        )
        each(
            outer,
            lambda step: outer_copy(
                mass_leaving, mass_arrived, outer_send2, outer_recv2, devices, me, step
            ).start(),
        )

    def await_group(block, last):
        for part in range(SOURCES):
            if last and part == SOURCES - 1:
                own.wait()
            else:
                tile_copy(block * SOURCES + 1 + part).wait_recv()

    def fill(block, short, weighted):
        sources = group_sources(devices, me, block)
        fill_deposit(group_fields(inbox, sources), short, weighted)

    await_group(0, False)
    fill(0, short_a, weighted_a)

    def deposit_pair(pair, carry):
        @pl.when(pair == RELAY_AT)
        def _():
            force_relay()

        await_group(2 * pair + 1, False)
        await_group(2 * pair + 2, False)
        fill(2 * pair + 1, short_b, weighted_b)
        add_deposit(short_a, weighted_a, total)
        fill(2 * pair + 2, short_a, weighted_a)
        add_deposit(short_b, weighted_b, total)
        return carry

    lax.fori_loop(0, pairs - 1, deposit_pair, 0)
    await_group(groups - 1, True)
    fill(groups - 1, short_b, weighted_b)
    add_deposit(short_a, weighted_a, total)
    add_deposit(short_b, weighted_b, total)

    spread_deposit(total, wide)
    flipped = jnp.transpose(wide[...])
    density[...] = flipped[0 : levels * SIDE, 0:CELLS]
    beyond = flipped[levels * SIDE : levels * SIDE + levels, :]
    edge = iota((levels * SIDE, 128), 1) < 65
    upper = jnp.where(edge, flipped[0 : levels * SIDE, CELLS:WIDE], 0.0)
    mass_gathered[lax.rem(me, INNER)] = upper + fold(beyond, F32, HIGHEST)
    each(
        INNER, lambda step: inner_copy(mass_gathered, inner_send2, inner_recv2, me, step).start()
    )

    each(
        outer,
        lambda step: outer_copy(
            force_leaving, force_arrived, outer_send, outer_recv, devices, me, step
        ).wait(),
    )
    for level in range(levels):
        table[level * depth : (level + 1) * depth, CELLS:WIDE] = final_table(
            near, 0, force_arrived, level, depth, me, BF16
        )
    beyond = unfold(table[0:rows, CELLS:WIDE], BF16, None)
    beyond.append(jnp.zeros((16 - len(beyond), WIDE), F32))
    table[rows : rows + 16, :] = jnp.concatenate(beyond, axis=0).astype(BF16)

    def kick_copy(step):
        return back_copy(kicks, returned, kick_send, kick_recv, devices, me, step)

    def cross_of(block, cross):
        fill_cross(group_fields(inbox, group_sources(devices, me, block)), cross)

    def sample_of(block, cross):
        sources = group_sources(devices, me, block)
        sample(group_fields(inbox, sources), sources, table, cross, kicks)

    def send_group(block, last):
        for part in range(SOURCES - 1 if last else SOURCES):
            kick_copy(block * SOURCES + 1 + part).start()

    cross_of(0, cross_a)

    def sample_pair(pair, carry):
        @pl.when(pair == RELAY_AT)
        def _():
            mass_relay()

        cross_of(2 * pair + 1, cross_b)
        sample_of(2 * pair, cross_a)
        cross_of(2 * pair + 2, cross_a)
        sample_of(2 * pair + 1, cross_b)
        send_group(2 * pair, False)
        send_group(2 * pair + 1, False)
        return carry

    lax.fori_loop(0, pairs - 1, sample_pair, 0)
    cross_of(groups - 1, cross_b)
    sample_of(groups - 2, cross_a)
    sample_of(groups - 1, cross_b)
    send_group(groups - 2, False)
    send_group(groups - 1, True)
    kept = pltpu.make_async_copy(kicks.at[block_rows(me)], returned.at[block_rows(me)], own_sem)
    kept.start()

    picks = slot_picks(owner_ref, count_ref[0], False)
    each(
        outer,
        lambda step: outer_copy(
            mass_leaving, mass_arrived, outer_send2, outer_recv2, devices, me, step
        ).wait(),
    )
    rims = jnp.concatenate(
        [final_table(near, levels, mass_arrived, level, SIDE, me, F32) for level in range(levels)],
        axis=0,
    )
    beyond = unfold(rims, F32, HIGHEST)
    first_row = iota((SIDE, 1), 0) == 0
    low = [
        rims[level * SIDE : (level + 1) * SIDE, :]
        + jnp.where(first_row, beyond[level][:, CELLS:WIDE], 0.0)
        for level in range(levels)
    ]
    added = jnp.dot(
        jnp.concatenate(low, axis=0),
        plane_pick(F32, True),
        preferred_element_type=F32,
        precision=HIGHEST,
    )
    for level in range(levels):
        at = slice(level * SIDE, (level + 1) * SIDE)
        density[at, :] += added[at, :] + jnp.where(first_row, beyond[level][:, 0:CELLS], 0.0)

    all_blocks(outbox, inbox, tile_send, tile_recv.at[0], devices, me).wait_send()
    kept.wait()
    all_blocks(kicks, returned, kick_send, kick_recv, devices, me).wait()
    parts = []
    for order in range(2):
        columns = [returned[pl.ds(order * 4 + axis, devices, stride=8), :] for axis in range(3)]
        parts.append(jnp.concatenate(columns, axis=1))
    mine = jnp.dot(
        picks, jnp.concatenate(parts, axis=0), preferred_element_type=F32, precision=HIGHEST
    )
    for axis in range(3):
        kick[axis] = mine[:, axis * 128 : (axis + 1) * 128]


def on_device(
    tile_mass, tile_frac, tile_cell, tile_level, tile_owner, tile_count, box_owner, force_field
):
    devices = lax.axis_size("boxes")
    levels = box_owner.shape[0]
    tiles, width = tile_mass.shape
    rows = levels * 3 * SIDE
    outer = devices // INNER
    shape = jax.ShapeDtypeStruct
    vmem = pl.BlockSpec(memory_space=pltpu.VMEM)
    smem = pl.BlockSpec(memory_space=pltpu.SMEM)
    dma = pltpu.SemaphoreType.DMA
    blocks = pltpu.VMEM((devices * 8, width), F32)
    spread_rows = CHUNKS * 2 * SIDE + 16
    density, kick = pl.pallas_call(
        functools.partial(kernel, devices, levels),
        out_shape=(shape((levels * SIDE, CELLS), F32), shape((3, tiles, width), F32)),
        in_specs=[smem] + [vmem] * 7,
        out_specs=(vmem, vmem),
        scratch_shapes=[
            blocks,
            blocks,
            blocks,
            blocks,
            pltpu.VMEM((2 * levels, devices, 128), F32),
            pltpu.VMEM((INNER, rows, 128), BF16),
            pltpu.VMEM((outer, rows, 128), BF16),
            pltpu.VMEM((outer, rows, 128), BF16),
            pltpu.VMEM((INNER, levels * SIDE, 128), F32),
            pltpu.VMEM((outer, levels * SIDE, 128), F32),
            pltpu.VMEM((outer, levels * SIDE, 128), F32),
            pltpu.VMEM((rows + 16, WIDE), BF16),
            pltpu.VMEM((WIDE, LANES), BF16),
            pltpu.VMEM((WIDE, LANES), BF16),
            pltpu.VMEM((SHORT + 16, LANES), BF16),
            pltpu.VMEM((SHORT + 16, LANES), BF16),
            pltpu.VMEM((spread_rows, LANES), BF16),
            pltpu.VMEM((spread_rows, LANES), BF16),
            pltpu.VMEM((SHORT + 16, 256), F32),
            pltpu.VMEM((WIDE, 128), F32),
            dma,
            dma,
            dma((devices - 1,)),
            dma,
            dma,
            dma((INNER - 1,)),
            dma((INNER - 1,)),
            dma((outer - 1,)),
            dma((outer - 1,)),
            dma((INNER - 1,)),
            dma((INNER - 1,)),
            dma((outer - 1,)),
            dma((outer - 1,)),
        ],
        compiler_params=pltpu.CompilerParams(
            collective_id=0, has_side_effects=True, vmem_limit_bytes=48 << 20
        ),
        name="deposit_and_sample",
    )(
        tile_count,
        tile_owner.reshape(1, tiles),
        box_owner,
        tile_mass,
        jnp.transpose(tile_frac, (1, 0, 2)),
        tile_cell,
        tile_level,
        force_field.reshape(rows, CELLS),
    )
    return (density.reshape(levels, SIDE, CELLS), jnp.transpose(kick, (1, 0, 2)))


def solution(mesh):
    in_specs = (
        P("boxes", None),
        P("boxes", None, None),
        P("boxes", None),
        P("boxes", None),
        P("boxes", None),
        P("boxes"),
        P(),
        P(None, None, "boxes", None),
    )
    out_specs = (P(None, "boxes", None), P("boxes", None, None))
    return jax.shard_map(
        on_device, mesh=mesh, in_specs=in_specs, out_specs=out_specs, check_vma=False
    )
```

time: 130 us -> 76.1 us (0.59)
  Pallas kernels: 122 us -> 68 us
  local copies, waits for them, and re-layouts: 2.57 us -> 6.49 us
  other arithmetic: 3.89 us -> 0 us
    pallas_call x3 -> x1, Pallas kernels: 122 us -> 68 us  [on_device(): pl.pallas_call(functools.partial(kernel, devices, levels), out_shape=(sha...]
    unnamed x17 -> x16, local copies, waits for them, and re-layouts: 2.56 us -> 6.49 us
    reduce_sum x2 -> x0, other arithmetic: 2.62 us -> none  [the longest x1 1.83 us: rim_sources(): jnp.sum(jnp.where(box[..., None] == places, box_owner[:, None, None, :],...]
where the time goes in v1:
time: 76.1 us; the launch traced here: 75.8 us
  Pallas kernels  68 us (89%)
  local copies, waits for them, and re-layouts  6.49 us (9%)
  between operations  1.31 us (2%)
    pallas_call x1, Pallas kernels, on_device(): pl.pallas_call(functools.partial(kernel, devices, levels), out_shape=(sha...  68 us
    unnamed x16, local copies, waits for them, and re-layouts  6.49 us

profile of v1, /device:TPU:1, one launch (start us, length us, event | category | flops | bytes accessed | tf_op | source)
XLA Modules:
  0.0 75.8 jit_solution(17558684633010836641)
XLA Ops:
  1.3 0.0 copy-start.5
  1.3 0.0 copy-start.6
  1.3 0.7 copy-done.5
  2.0 0.0 copy-done.6
  2.0 0.0 copy-start
  2.0 1.0 %copy-done = bf16[2,3,32,1024]{3,2,1,0:T(8,128)(2,1)S(1)} copy-done((bf16[2,3,32,1024]{3,2,1,0:T(8,128)(2,1)S(1)}, bf16[2,3,32,1024]{3,2,1,0:T(8,128)(2,1)}, u32[]{:S(2)}) %copy-start) | copy-done | bytes 393240
  3.0 0.0 copy-start.1
  3.0 0.9 %copy-done.1 = f32[128,3,128]{2,0,1:T(8,128)S(1)} copy-done((f32[128,3,128]{2,0,1:T(8,128)S(1)}, f32[128,3,128]{2,0,1:T(8,128)}, u32[]{:S(2)}) %copy-start.1) | copy-done | bytes 196632
  3.9 0.0 copy-start.2
  3.9 0.8 %copy-done.2 = f32[128,128]{1,0:T(8,128)S(1)} copy-done((f32[128,128]{1,0:T(8,128)S(1)}, f32[128,128]{1,0:T(8,128)}, u32[]{:S(2)}) %copy-start.2) | copy-done | bytes 65560
  4.7 0.0 copy-start.3
  4.7 0.8 %copy-done.3 = s32[128,128]{1,0:T(8,128)S(1)} copy-done((s32[128,128]{1,0:T(8,128)S(1)}, s32[128,128]{1,0:T(8,128)}, u32[]{:S(2)}) %copy-start.3) | copy-done | bytes 65560
  5.6 0.0 copy-start.4
  5.6 0.8 %copy-done.4 = s32[128,128]{1,0:T(8,128)S(1)} copy-done((s32[128,128]{1,0:T(8,128)S(1)}, s32[128,128]{1,0:T(8,128)}, u32[]{:S(2)}) %copy-start.4) | copy-done | bytes 65560
  6.4 68.0 %deposit_and_sample.1 = (f32[64,1024]{1,0:T(8,128)S(1)}, f32[3,128,128]{2,1,0:T(8,128)S(1)}) custom-call(s32[1]{0:T(128)S(6)} %copy.12.count_ref, s32[1,128]{1,0:T(1,128)S(1)} %bitcast.9, s32[2,128]{1,0:T(2,128)S(1)} %copy-done.5, f32[128,128]{1,0:T(8,128)S(1)} %copy-done.2, f32[3,128,128]{2,1,0:T(8,128)S(1)} %bitcast.8, s32[128,128]{1,0:T(8,128)S(1)} %copy-done.3, ...), custom_call_target="tpu_custom_call" | custom-call | tf_op jit(solution)/shard_map/deposit_and_sample/pallas_call | solution.py:631
  74.4 0.7 copy.13
  75.1 0.7 copy.14
Async XLA Ops:
  1.3 0.7 copy-start.5
  1.3 0.7 copy-start.6
  2.0 1.0 %copy-start = (bf16[2,3,32,1024]{3,2,1,0:T(8,128)(2,1)S(1)}, bf16[2,3,32,1024]{3,2,1,0:T(8,128)(2,1)}, u32[]{:S(2)}) copy-start(bf16[2,3,32,1024]{3,2,1,0:T(8,128)(2,1)} %param.15) | copy-start | bytes 1179652
  3.0 0.9 %copy-start.1 = (f32[128,3,128]{2,0,1:T(8,128)S(1)}, f32[128,3,128]{2,0,1:T(8,128)}, u32[]{:S(2)}) copy-start(f32[128,3,128]{2,0,1:T(8,128)} %param.9) | copy-start | bytes 589828
  3.9 0.8 %copy-start.2 = (f32[128,128]{1,0:T(8,128)S(1)}, f32[128,128]{1,0:T(8,128)}, u32[]{:S(2)}) copy-start(f32[128,128]{1,0:T(8,128)} %mass_ref.1) | copy-start | bytes 196612
  4.7 0.8 %copy-start.3 = (s32[128,128]{1,0:T(8,128)S(1)}, s32[128,128]{1,0:T(8,128)}, u32[]{:S(2)}) copy-start(s32[128,128]{1,0:T(8,128)} %cell_ref.1) | copy-start | bytes 196612
  5.6 0.8 %copy-start.4 = (s32[128,128]{1,0:T(8,128)S(1)}, s32[128,128]{1,0:T(8,128)}, u32[]{:S(2)}) copy-start(s32[128,128]{1,0:T(8,128)} %level_ref.1) | copy-start | bytes 196612

commit v2 on v1

--- a/solution.py
+++ b/solution.py
@@ -24,7 +24,8 @@
 CHUNK = 11
 CHUNKS = 3
 SHORT = (CHUNK + 1) * SIDE
-RELAY_AT = 3
+FORCE_STAGES = (4, 8, 12)
+MASS_STAGES = (3, 7, 10)
 
 direction_table = np.array(
     [[1, 0, 0], [0, 1, 0], [0, 0, 1], [1, 1, 0], [1, 0, 1], [0, 1, 1], [1, 1, 1]], dtype=np.int32
@@ -39,47 +40,54 @@
     return jnp.where(mask, 1.0, 0.0).astype(dtype)
 
 
-def kind_of(lane):
-    kind = jnp.where(lane < 32, 1, jnp.where(lane < 64, 2, -1))
-    kind = jnp.where(lane == 64, 5, jnp.where(lane == 65, 3, kind))
-    kind = jnp.where(lane == 66, 4, jnp.where(lane == 67, 6, kind))
-    return jnp.where(lane >= 96, 0, kind)
-
-
-def fold_target(lane):
-    target = jnp.where(lane < CELLS, 96 + lane % SIDE, -1)
-    target = jnp.where((lane >= CELLS) & (lane < CELLS + 32), 65, target)
-    target = jnp.where((lane >= CELLS + 32) & (lane < CELLS + 64), 66, target)
-    return jnp.where(lane == CELLS + 64, 67, target)
-
-
-def fold_row(lane):
-    row = jnp.where(lane < CELLS, lane // SIDE, -1)
-    row = jnp.where((lane >= CELLS) & (lane < CELLS + 32), lane - CELLS, row)
-    row = jnp.where((lane >= CELLS + 32) & (lane < CELLS + 64), lane - CELLS - 32, row)
-    return jnp.where(lane == CELLS + 64, 0, row)
-
-
-def fold(rows, dtype, precision):
-    amount = rows.shape[0]
-    shape = (SIDE, WIDE)
-    own = fold_row(iota(shape, 1)) == iota(shape, 0)
-    parts = [jnp.where(own, rows[place : place + 1, :], 0.0) for place in range(amount)]
-    picked = jnp.concatenate(parts, axis=0).astype(dtype)
-    pick = ones_at(fold_target(iota((WIDE, 128), 0)) == iota((WIDE, 128), 1), dtype)
-    return jnp.dot(picked, pick, preferred_element_type=F32, precision=precision)
-
-
-def unfold(table, dtype, precision):
-    pick = ones_at(fold_target(iota((128, WIDE), 1)) == iota((128, WIDE), 0), dtype)
-    spread = jnp.dot(table, pick, preferred_element_type=F32, precision=precision)
-    shape = (SIDE, WIDE)
-    own = fold_row(iota(shape, 1)) == iota(shape, 0)
-    rows = []
-    for place in range(table.shape[0] // SIDE):
-        part = jnp.where(own, spread[place * SIDE : (place + 1) * SIDE, :], 0.0)
-        rows.append(jnp.sum(part, axis=0, keepdims=True))
-    return rows
+def kind_of(value, parts):
+    slab = value // 8
+    group = slab // 5
+    part = slab % 5
+    kind = jnp.where(part == 3, 5, part)
+    corner = value % 8
+    kind = jnp.where(part == 4, jnp.where(corner == 0, 3, jnp.where(corner == 1, 4, 6)), kind)
+    return group // parts, kind
+
+
+def pack_rims(edges, fronts):
+    lane = iota((8, 128), 1)
+    row = iota((8, 128), 0)
+    slabs = []
+    for place, front in enumerate(fronts):
+        pieces = [front[:, 128 * part : 128 * part + 128] for part in range(8)]
+        slabs.append(jnp.concatenate(pieces, axis=0))
+        for start in (0, 32, 64):
+            total = None
+            for part in range(4):
+                at = place * SIDE + part * 8
+                moved = pltpu.roll(edges[at : at + 8, :], (32 * part - start) % 128, 1)
+                total = moved if total is None else jnp.where(lane >= 32 * part, moved, total)
+            slabs.append(total)
+        last = jnp.broadcast_to(front[:, CELLS:WIDE], (8, 128))
+        corners = jnp.where(row == 0, last, pltpu.roll(last, 96, 1))
+        slabs.append(jnp.where(row == 2, pltpu.roll(last, 64, 1), corners))
+    return jnp.concatenate(slabs, axis=0)
+
+
+def unpack_rims(values, amount):
+    lane = iota((8, 128), 1)
+    edges, fronts = [], []
+    for place in range(amount):
+        at = place * 40
+        pieces = [values[at + part : at + part + 1, :] for part in range(8)]
+        plane_y, plane_z, line = [values[at + 8 * n : at + 8 * n + 8, :] for n in (1, 2, 3)]
+        for part in range(4):
+            moved = pltpu.roll(plane_z, (32 - 32 * part) % 128, 1)
+            moved = jnp.where(lane < 32, pltpu.roll(plane_y, (-32 * part) % 128, 1), moved)
+            moved = jnp.where(lane == 64, pltpu.roll(line, (64 - 32 * part) % 128, 1), moved)
+            edges.append(jnp.where(lane <= 64, moved, 0.0))
+        corners = values[at + 32 : at + 40, :]
+        first = jnp.where(lane < 32, corners, 0.0)[0:1, :]
+        second = jnp.where((lane >= 32) & (lane < 64), pltpu.roll(corners, 32, 1), 0.0)[1:2, :]
+        third = jnp.where(lane == 64, pltpu.roll(corners, 64, 1), 0.0)[2:3, :]
+        fronts.append(jnp.concatenate(pieces + [first + second + third], axis=1))
+    return jnp.concatenate(edges, axis=0), fronts
 
 
 def plane_pick(dtype, flip):
@@ -118,7 +126,6 @@
     places = iota(square, 0).astype(F32).astype(BF16)
     box = jnp.dot(hot, places, preferred_element_type=F32).astype(jnp.int32)
     at = [box // (lat_y * LAT_Z), box // LAT_Z % lat_y, box % LAT_Z]
-    kind = kind_of(iota(square, 1))
     found = []
     for sign in (1, -1):
         hots = []
@@ -130,12 +137,22 @@
             wanted = (near[0] * lat_y + near[1]) * LAT_Z + near[2]
             hots.append(ones_at(wanted == iota(square, 1), BF16))
         owners = jnp.dot(jnp.concatenate(hots, axis=0), down, preferred_element_type=F32)
-        total = jnp.zeros(square, F32)
+        found.append(ones_at(owners == iota(owners.shape, 1).astype(F32), BF16))
+    return found
+
+
+def choose(hots, values, parts, devices):
+    levels = hots.shape[0] // (7 * devices)
+    width = values.shape[1]
+    level_of, kind = kind_of(iota((1, width), 1), parts)
+    total = jnp.zeros((devices, width), F32)
+    for level in range(levels):
+        at = level * 7 * devices
+        found = jnp.dot(hots[at : at + 7 * devices, :], values, preferred_element_type=F32)
         for direction in range(7):
-            part = owners[direction * devices : (direction + 1) * devices, :]
-            total = jnp.where(kind == direction, part, total)
-        found.append(total)
-    return found
+            part = found[direction * devices : (direction + 1) * devices, :]
+            total = jnp.where((level_of == level) & (kind == direction), part, total)
+    return total
 
 
 def each(count, act):
@@ -186,61 +203,59 @@
     )
 
 
-def inner_copy(gathered, send, recv, me, step):
-    place = lax.rem(me, INNER)
-    peer = me - place + lax.rem(place + step, INNER)
-    return pltpu.make_async_remote_copy(
-        src_ref=gathered.at[place],
-        dst_ref=gathered.at[place],
-        send_sem=send.at[step - 1],
-        recv_sem=recv.at[step - 1],
-        device_id=(peer,),
-        device_id_type=MESH,
-    )
-
-
-def outer_copy(leaving, arrived, send, recv, devices, me, step):
-    outer = devices // INNER
-    row = me // INNER
-    other = lax.rem(row + step, outer)
-    return pltpu.make_async_remote_copy(
-        src_ref=leaving.at[other],
-        dst_ref=arrived.at[row],
-        send_sem=send.at[step - 1],
-        recv_sem=recv.at[step - 1],
-        device_id=(other * INNER + lax.rem(me, INNER),),
-        device_id_type=MESH,
-    )
-
-
-def choose(tables, wanted, level, depth, dtype):
-    total = None
-    for place in range(tables.shape[0]):
-        keep = ones_at(wanted == float(place), dtype)
-        part = tables[place, level * depth : (level + 1) * depth, :] * keep
-        total = part if total is None else total + part
-    return total
-
-
-def relay(near, first, gathered, leaving, arrived, outer, levels, depth, me, dtype):
-    place, row = lax.rem(me, INNER), me // INNER
-
-    def body(other, carry):
-        for level in range(levels):
-            wanted = near[first + level, pl.ds(other * INNER + place, 1), :]
-            wanted = wanted - INNER * jnp.floor(wanted / INNER)
-            leaving[other, level * depth : (level + 1) * depth, :] = choose(
-                gathered, wanted, level, depth, dtype
-            )
-        return carry
-
-    lax.fori_loop(0, outer, body, 0)
-    arrived[row] = leaving[row]
-
-
-def final_table(near, first, arrived, level, depth, me, dtype):
-    wanted = jnp.floor(near[first + level, pl.ds(me, 1), :] / INNER)
-    return choose(arrived, wanted, level, depth, dtype)
+def rim_hops(source, middle, target, sems, devices, me):
+    rows = devices // INNER
+    row, place = me // INNER, lax.rem(me, INNER)
+
+    def first(step):
+        other = lax.rem(place + step, INNER)
+        return pltpu.make_async_remote_copy(
+            src_ref=source.at[:, other],
+            dst_ref=middle.at[place],
+            send_sem=sems.at[0],
+            recv_sem=sems.at[1],
+            device_id=(row * INNER + other,),
+            device_id_type=MESH,
+        )
+
+    def second(step):
+        other = lax.rem(row + step, rows)
+        return pltpu.make_async_remote_copy(
+            src_ref=middle.at[:, other],
+            dst_ref=target.at[row],
+            send_sem=sems.at[2],
+            recv_sem=sems.at[3],
+            device_id=(other * INNER + place,),
+            device_id_type=MESH,
+        )
+
+    def start():
+        each(INNER, lambda step: first(step).start())
+        middle[place] = source[:, place]
+
+    def forward():
+        pltpu.make_async_remote_copy(
+            src_ref=middle.at[pl.ds(0, INNER - 1)],
+            dst_ref=middle.at[pl.ds(0, INNER - 1)],
+            send_sem=sems.at[0],
+            recv_sem=sems.at[1],
+            device_id=(row * INNER + lax.rem(place + 1, INNER),),
+            device_id_type=MESH,
+        ).wait()
+        each(rows, lambda step: second(step).start())
+        target[row] = middle[:, row]
+
+    def finish():
+        pltpu.make_async_remote_copy(
+            src_ref=target.at[pl.ds(0, rows - 1)],
+            dst_ref=target.at[pl.ds(0, rows - 1)],
+            send_sem=sems.at[2],
+            recv_sem=sems.at[3],
+            device_id=(lax.rem(row + 1, rows) * INNER + place,),
+            device_id_type=MESH,
+        ).wait()
+
+    return start, forward, finish
 
 
 def hat(coord, rows, start):
@@ -345,24 +360,33 @@
     count_ref,
     owner_ref,
     box_owner,
-    mass_ref,
-    frac_ref,
-    cell_ref,
-    level_ref,
-    force_ref,
+    mass_in,
+    frac_in,
+    cell_in,
+    level_in,
+    force_in,
     density,
     kick,
     outbox,
     inbox,
     kicks,
     returned,
-    near,
-    force_gathered,
-    force_leaving,
-    force_arrived,
-    mass_gathered,
-    mass_leaving,
-    mass_arrived,
+    mass_ref,
+    frac_ref,
+    cell_ref,
+    level_ref,
+    force_ref,
+    hots,
+    force_out,
+    force_spread,
+    force_next,
+    force_last,
+    mass_out,
+    mass_spread,
+    mass_next,
+    mass_last,
+    force_middle,
+    mass_middle,
     table,
     cross_a,
     cross_b,
@@ -377,22 +401,29 @@
     tile_recv,
     kick_send,
     kick_recv,
-    inner_send,
-    inner_recv,
-    outer_send,
-    outer_recv,
-    inner_send2,
-    inner_recv2,
-    outer_send2,
-    outer_recv2,
+    load_sem,
+    rim_sems,
 ):
     me = lax.axis_index("boxes")
-    outer = devices // INNER
     depth = 3 * SIDE
     rows = levels * depth
     groups = devices // SOURCES
     pairs = groups // 2
 
+    loads = [
+        pltpu.make_async_copy(source, target, load_sem.at[place])
+        for place, (source, target) in enumerate(
+            [
+                (mass_in, mass_ref),
+                (frac_in, frac_ref),
+                (cell_in, cell_ref),
+                (level_in, level_ref),
+                (force_in, force_ref),
+            ]
+        )
+    ]
+    for load in loads:
+        load.start()
     barrier = pltpu.get_barrier_semaphore()
     each(
         devices,
@@ -402,6 +433,8 @@
     )
 
     picks = slot_picks(owner_ref, count_ref[0], True)
+    for load in loads[:4]:
+        load.wait()
     cell = cell_ref[...]
     digits = [cell // CELLS, cell // SIDE % SIDE, cell % SIDE]
     fields = [jnp.where(level_ref[...] == 0, mass_ref[...], -mass_ref[...])]
@@ -415,73 +448,88 @@
             part = packed[order * devices : (order + 1) * devices, field * 128 : field * 128 + 128]
             outbox[pl.ds(order * 4 + field, devices, stride=8), :] = part
 
+    pl.semaphore_wait(barrier, devices - 1)
+
+    force_hops = [
+        rim_hops(force_out, force_middle.at[0], force_spread, rim_sems.at[0], devices, me),
+        rim_hops(force_next, force_middle.at[1], force_last, rim_sems.at[1], devices, me),
+    ]
+    mass_hops = [
+        rim_hops(mass_out, mass_middle.at[0], mass_spread, rim_sems.at[2], devices, me),
+        rim_hops(mass_next, mass_middle.at[1], mass_last, rim_sems.at[3], devices, me),
+    ]
+
+    def tile_copy(step):
+        group = (step - 1) // SOURCES
+        return block_copy(outbox, inbox, tile_send, tile_recv.at[group], devices, me, step)
+
+    each(devices, lambda step: tile_copy(step).start())
+    own = pltpu.make_async_copy(outbox.at[block_rows(me)], inbox.at[block_rows(me)], own_sem)
+    own.start()
+
+    loads[4].wait()
     force = force_ref[...]
-    planes = jnp.dot(force, plane_pick(BF16, False), preferred_element_type=F32)
+    edges = jnp.dot(force, plane_pick(BF16, False), preferred_element_type=F32)
     fronts = []
     for place in range(levels * 3):
         at = place * SIDE
         front = force_ref[at : at + 16, :].astype(F32)[0:1, :]
-        fronts.append(jnp.concatenate([front, planes[at : at + 1, :]], axis=1))
-    lower = planes + fold(jnp.concatenate(fronts, axis=0), BF16, None)
-    force_gathered[lax.rem(me, INNER)] = lower.astype(BF16)
-
-    pl.semaphore_wait(barrier, devices - 1)
-    each(
-        INNER, lambda step: inner_copy(force_gathered, inner_send, inner_recv, me, step).start()
-    )
-
-    def tile_copy(step):
-        return block_copy(outbox, inbox, tile_send, tile_recv.at[step - 1], devices, me, step)
-
-    each(devices, lambda step: tile_copy(step).start())
-    own = pltpu.make_async_copy(outbox.at[block_rows(me)], inbox.at[block_rows(me)], own_sem)
-    own.start()
+        fronts.append(jnp.concatenate([front, edges[at : at + 1, :]], axis=1))
+    values = pack_rims(edges, fronts)
+    values = jnp.concatenate([values, jnp.zeros((256 - values.shape[0], 128), F32)], axis=0)
+    for half in range(2):
+        block = jnp.transpose(values[half * 128 : half * 128 + 128, :])
+        force_out[:, :, half, :] = block.reshape(devices // INNER, INNER, 128)
+    force_hops[0][0]()
 
     for level in range(levels):
-        forward, backward = rim_sources(box_owner, level, devices)
-        near[level] = forward
-        near[levels + level] = backward
+        ways = rim_sources(box_owner, level, devices)
+        for way in range(2):
+            hots[pl.ds((way * levels + level) * 7 * devices, 7 * devices), :] = ways[way]
     table[0:rows, 0:CELLS] = force
-    cross_a[...] = jnp.zeros_like(cross_a)
-    cross_b[...] = jnp.zeros_like(cross_b)
+    blank = jnp.zeros((WIDE - CELLS - 80, LANES), BF16)
+    cross_a[CELLS + 80 : WIDE, :] = blank
+    cross_b[CELLS + 80 : WIDE, :] = blank
     total[...] = jnp.zeros_like(total)
     kicks[...] = jnp.zeros_like(kicks)
 
     def force_relay():
-        each(
-            INNER, lambda step: inner_copy(force_gathered, inner_send, inner_recv, me, step).wait()
+        force_hops[0][2]()
+        values = jnp.concatenate(
+            [force_spread[:, :, half, :].reshape(devices, 128) for half in range(2)], axis=1
         )
-        relay(
-            near, 0, force_gathered, force_leaving, force_arrived, outer, levels, depth, me, BF16
-        )
-        each(
-            outer,
-            lambda step: outer_copy(
-                force_leaving, force_arrived, outer_send, outer_recv, devices, me, step
-            ).start(),
-        )
+        chosen = choose(hots[0 : levels * 7 * devices, :], values.astype(BF16), 3, devices)
+        for half in range(2):
+            block = chosen[:, half * 128 : half * 128 + 128]
+            force_next[:, :, half, :] = block.reshape(devices // INNER, INNER, 128)
+        force_hops[1][0]()
 
     def mass_relay():
-        each(
-            INNER,
-            lambda step: inner_copy(mass_gathered, inner_send2, inner_recv2, me, step).wait(),
-        )
-        relay(
-            near, levels, mass_gathered, mass_leaving, mass_arrived, outer, levels, SIDE, me, F32
-        )
-        each(
-            outer,
-            lambda step: outer_copy(
-                mass_leaving, mass_arrived, outer_send2, outer_recv2, devices, me, step
-            ).start(),
-        )
+        mass_hops[0][2]()
+        values = mass_spread[:, :, 0, :].reshape(devices, 128)
+        high = values.astype(BF16)
+        rest = (values - high.astype(F32)).astype(BF16)
+        way = hots[levels * 7 * devices : 2 * levels * 7 * devices, :]
+        chosen = choose(way, high, 1, devices) + choose(way, rest, 1, devices)
+        mass_next[:, :, 0, :] = chosen.reshape(devices // INNER, INNER, 128)
+        mass_hops[1][0]()
+
+    def stages(pair, at, acts):
+        for place, act in zip(at, acts):
+            pl.when(pair == place)(act)
 
     def await_group(block, last):
-        for part in range(SOURCES):
-            if last and part == SOURCES - 1:
-                own.wait()
-            else:
-                tile_copy(block * SOURCES + 1 + part).wait_recv()
+        if last:
+            own.wait()
+        amount = (SOURCES - 1 if last else SOURCES) * 8
+        pltpu.make_async_remote_copy(
+            src_ref=outbox.at[pl.ds(0, amount)],
+            dst_ref=inbox.at[pl.ds(0, amount)],
+            send_sem=tile_send,
+            recv_sem=tile_recv.at[block],
+            device_id=(lax.rem(me + 1, devices),),
+            device_id_type=MESH,
+        ).wait_recv()
 
     def fill(block, short, weighted):
         sources = group_sources(devices, me, block)
@@ -491,10 +539,7 @@
     fill(0, short_a, weighted_a)
 
     def deposit_pair(pair, carry):
-        @pl.when(pair == RELAY_AT)
-        def _():
-            force_relay()
-
+        stages(pair, FORCE_STAGES, (force_hops[0][1], force_relay, force_hops[1][1]))
         await_group(2 * pair + 1, False)
         await_group(2 * pair + 2, False)
         fill(2 * pair + 1, short_b, weighted_b)
@@ -513,26 +558,23 @@
     flipped = jnp.transpose(wide[...])
     density[...] = flipped[0 : levels * SIDE, 0:CELLS]
     beyond = flipped[levels * SIDE : levels * SIDE + levels, :]
-    edge = iota((levels * SIDE, 128), 1) < 65
-    upper = jnp.where(edge, flipped[0 : levels * SIDE, CELLS:WIDE], 0.0)
-    mass_gathered[lax.rem(me, INNER)] = upper + fold(beyond, F32, HIGHEST)
-    each(
-        INNER, lambda step: inner_copy(mass_gathered, inner_send2, inner_recv2, me, step).start()
-    )
-
-    each(
-        outer,
-        lambda step: outer_copy(
-            force_leaving, force_arrived, outer_send, outer_recv, devices, me, step
-        ).wait(),
-    )
-    for level in range(levels):
-        table[level * depth : (level + 1) * depth, CELLS:WIDE] = final_table(
-            near, 0, force_arrived, level, depth, me, BF16
-        )
-    beyond = unfold(table[0:rows, CELLS:WIDE], BF16, None)
-    beyond.append(jnp.zeros((16 - len(beyond), WIDE), F32))
-    table[rows : rows + 16, :] = jnp.concatenate(beyond, axis=0).astype(BF16)
+    values = pack_rims(
+        flipped[0 : levels * SIDE, CELLS:WIDE],
+        [beyond[level : level + 1, :] for level in range(levels)],
+    )
+    values = jnp.concatenate([values, jnp.zeros((128 - values.shape[0], 128), F32)], axis=0)
+    mass_out[:, :, 0, :] = jnp.transpose(values).reshape(devices // INNER, INNER, 128)
+    mass_hops[0][0]()
+
+    force_hops[1][2]()
+    values = jnp.concatenate(
+        [jnp.transpose(force_last[:, :, half, :].reshape(devices, 128)) for half in range(2)],
+        axis=0,
+    )
+    edges, fronts = unpack_rims(values, levels * 3)
+    table[0:rows, CELLS:WIDE] = edges.astype(BF16)
+    fronts.append(jnp.zeros((16 - len(fronts), WIDE), F32))
+    table[rows : rows + 16, :] = jnp.concatenate(fronts, axis=0).astype(BF16)
 
     def kick_copy(step):
         return back_copy(kicks, returned, kick_send, kick_recv, devices, me, step)
@@ -551,10 +593,7 @@
     cross_of(0, cross_a)
 
     def sample_pair(pair, carry):
-        @pl.when(pair == RELAY_AT)
-        def _():
-            mass_relay()
-
+        stages(pair, MASS_STAGES, (mass_hops[0][1], mass_relay, mass_hops[1][1]))
         cross_of(2 * pair + 1, cross_b)
         sample_of(2 * pair, cross_a)
         cross_of(2 * pair + 2, cross_a)
@@ -573,21 +612,13 @@
     kept.start()
 
     picks = slot_picks(owner_ref, count_ref[0], False)
-    each(
-        outer,
-        lambda step: outer_copy(
-            mass_leaving, mass_arrived, outer_send2, outer_recv2, devices, me, step
-        ).wait(),
-    )
-    rims = jnp.concatenate(
-        [final_table(near, levels, mass_arrived, level, SIDE, me, F32) for level in range(levels)],
-        axis=0,
-    )
-    beyond = unfold(rims, F32, HIGHEST)
+    mass_hops[1][2]()
+    values = jnp.transpose(mass_last[:, :, 0, :].reshape(devices, 128))
+    edges, fronts = unpack_rims(values, levels)
     first_row = iota((SIDE, 1), 0) == 0
     low = [
-        rims[level * SIDE : (level + 1) * SIDE, :]
-        + jnp.where(first_row, beyond[level][:, CELLS:WIDE], 0.0)
+        edges[level * SIDE : (level + 1) * SIDE, :]
+        + jnp.where(first_row, fronts[level][:, CELLS:WIDE], 0.0)
         for level in range(levels)
     ]
     added = jnp.dot(
@@ -598,7 +629,7 @@
     )
     for level in range(levels):
         at = slice(level * SIDE, (level + 1) * SIDE)
-        density[at, :] += added[at, :] + jnp.where(first_row, beyond[level][:, 0:CELLS], 0.0)
+        density[at, :] += added[at, :] + jnp.where(first_row, fronts[level][:, 0:CELLS], 0.0)
 
     all_blocks(outbox, inbox, tile_send, tile_recv.at[0], devices, me).wait_send()
     kept.wait()
@@ -621,7 +652,6 @@
     levels = box_owner.shape[0]
     tiles, width = tile_mass.shape
     rows = levels * 3 * SIDE
-    outer = devices // INNER
     shape = jax.ShapeDtypeStruct
     vmem = pl.BlockSpec(memory_space=pltpu.VMEM)
     smem = pl.BlockSpec(memory_space=pltpu.SMEM)
@@ -631,20 +661,27 @@
     density, kick = pl.pallas_call(
         functools.partial(kernel, devices, levels),
         out_shape=(shape((levels * SIDE, CELLS), F32), shape((3, tiles, width), F32)),
-        in_specs=[smem] + [vmem] * 7,
+        in_specs=[smem, vmem, vmem] + [pl.BlockSpec(memory_space=pl.ANY)] * 5,
         out_specs=(vmem, vmem),
         scratch_shapes=[
             blocks,
             blocks,
             blocks,
             blocks,
-            pltpu.VMEM((2 * levels, devices, 128), F32),
-            pltpu.VMEM((INNER, rows, 128), BF16),
-            pltpu.VMEM((outer, rows, 128), BF16),
-            pltpu.VMEM((outer, rows, 128), BF16),
-            pltpu.VMEM((INNER, levels * SIDE, 128), F32),
-            pltpu.VMEM((outer, levels * SIDE, 128), F32),
-            pltpu.VMEM((outer, levels * SIDE, 128), F32),
+            pltpu.VMEM((tiles, width), F32),
+            pltpu.VMEM((3, tiles, width), F32),
+            pltpu.VMEM((tiles, width), jnp.int32),
+            pltpu.VMEM((tiles, width), jnp.int32),
+            pltpu.VMEM((rows, CELLS), BF16),
+            pltpu.VMEM((2 * levels * 7 * devices, devices), BF16),
+        ]
+        + [pltpu.VMEM((devices // INNER, INNER, 2, 128), F32)] * 4
+        + [pltpu.VMEM((devices // INNER, INNER, 1, 128), F32)] * 4
+        + [
+            pltpu.VMEM((2, INNER, devices // INNER, 2, 128), F32),
+            pltpu.VMEM((2, INNER, devices // INNER, 1, 128), F32),
+        ]
+        + [
             pltpu.VMEM((rows + 16, WIDE), BF16),
             pltpu.VMEM((WIDE, LANES), BF16),
             pltpu.VMEM((WIDE, LANES), BF16),
@@ -656,20 +693,14 @@
             pltpu.VMEM((WIDE, 128), F32),
             dma,
             dma,
-            dma((devices - 1,)),
+            dma((devices // SOURCES,)),
             dma,
             dma,
-            dma((INNER - 1,)),
-            dma((INNER - 1,)),
-            dma((outer - 1,)),
-            dma((outer - 1,)),
-            dma((INNER - 1,)),
-            dma((INNER - 1,)),
-            dma((outer - 1,)),
-            dma((outer - 1,)),
+            dma((5,)),
+            dma((4, 4)),
         ],
         compiler_params=pltpu.CompilerParams(
-            collective_id=0, has_side_effects=True, vmem_limit_bytes=48 << 20
+            collective_id=0, has_side_effects=True, vmem_limit_bytes=60 << 20
         ),
         name="deposit_and_sample",
     )(

time: 76.1 us -> 70.8 us (0.930)
  local copies, waits for them, and re-layouts: 6.49 us -> 2.39 us
  Pallas kernels: 68 us -> 67 us
    unnamed x16 -> x4, local copies, waits for them, and re-layouts: 6.49 us -> 2.39 us
    pallas_call x1, Pallas kernels: 68 us -> 67 us  [on_device(): pl.pallas_call(functools.partial(kernel, devices, levels), out_shape=(sha...]
where the time goes in v2:
time: 70.8 us; the launch traced here: 70.7 us
  Pallas kernels  67 us (95%)
  local copies, waits for them, and re-layouts  2.39 us (3%)
  between operations  1.29 us (2%)
    pallas_call x1, Pallas kernels, on_device(): pl.pallas_call(functools.partial(kernel, devices, levels), out_shape=(sha...  67 us
    unnamed x4, local copies, waits for them, and re-layouts  2.39 us

profile of v2, /device:TPU:1, one launch (start us, length us, event | category | flops | bytes accessed | tf_op | source)
XLA Modules:
  0.0 70.7 jit_solution(7709618417159300252)
XLA Ops:
  1.3 67.0 %deposit_and_sample.1 = (f32[64,1024]{1,0:T(8,128)}, f32[3,128,128]{2,1,0:T(8,128)}) custom-call(s32[1]{0:T(128)S(6)} %copy.12.count_ref, s32[1,128]{1,0:T(1,128)} %bitcast.9, s32[2,128]{1,0:T(2,128)} %box_owner.1, f32[128,128]{1,0:T(8,128)} %mass_in.1, f32[3,128,128]{2,1,0:T(8,128)} %bitcast.8, s32[128,128]{1,0:T(8,128)} %cell_in.1, s32[128,128]{1,0:T(8,128)} %level_in.1, ...), custom_call_target="tpu_custom_call" | custom-call | tf_op jit(solution)/shard_map/deposit_and_sample/pallas_call | solution.py:661
  68.3 0.0 copy-start
  68.3 1.7 %copy.13 = f32[2,32,1024]{2,1,0:T(8,128)} copy(f32[2,32,1024]{2,1,0:T(8,128)} %bitcast.6) | data formatting | bytes 524288
  70.0 0.0 copy-done
  70.0 0.7 copy.14
Async XLA Ops:
  68.3 1.7 %copy-start = (f32[3,128,128]{2,1,0:T(8,128)S(1)}, f32[3,128,128]{2,1,0:T(8,128)}, u32[]{:S(2)}) copy-start(f32[3,128,128]{2,1,0:T(8,128)} %get-tuple-element.5) | copy-start | bytes 589828

commit v3 on v2

--- a/solution.py
+++ b/solution.py
@@ -9,7 +9,6 @@
 from jax.sharding import PartitionSpec as P
 
 MESH = pl.DeviceIdType.MESH
-HIGHEST = lax.Precision.HIGHEST
 F32 = jnp.float32
 BF16 = jnp.bfloat16
 LAT_X = 4
@@ -18,14 +17,13 @@
 CELLS = SIDE * SIDE
 WIDE = CELLS + 128
 INNER = 8
-SOURCES = 4
-GROUP = 2 * SOURCES
+GROUP = 2 * INNER
 LANES = GROUP * 128
 CHUNK = 11
 CHUNKS = 3
 SHORT = (CHUNK + 1) * SIDE
-FORCE_STAGES = (4, 8, 12)
-MASS_STAGES = (3, 7, 10)
+FORCE_STAGES = (4, 6)
+MASS_STAGES = (1, 3, 5)
 
 direction_table = np.array(
     [[1, 0, 0], [0, 1, 0], [0, 0, 1], [1, 1, 0], [1, 0, 1], [0, 1, 1], [1, 1, 1]], dtype=np.int32
@@ -38,6 +36,17 @@
 
 def ones_at(mask, dtype):
     return jnp.where(mask, 1.0, 0.0).astype(dtype)
+
+
+def exact_dot(picks, values):
+    width = values.shape[1]
+    high = values.astype(BF16)
+    rest = values - high.astype(F32)
+    middle = rest.astype(BF16)
+    low = (rest - middle.astype(F32)).astype(BF16)
+    parts = jnp.concatenate([high, middle, low], axis=1)
+    found = jnp.dot(picks, parts, preferred_element_type=F32)
+    return (found[:, 0:width] + found[:, width : 2 * width]) + found[:, 2 * width : 3 * width]
 
 
 def kind_of(value, parts):
@@ -114,7 +123,7 @@
         rank = jnp.sum(earlier, axis=1, keepdims=True)
         fits = (down == second) & (first < count)
     picks = [jnp.where(fits & (rank == float(order)), 1.0, 0.0) for order in range(2)]
-    return jnp.concatenate(picks, axis=0 if by_slot else 1)
+    return jnp.concatenate(picks, axis=0 if by_slot else 1).astype(BF16)
 
 
 def rim_sources(box_owner, level, devices):
@@ -144,7 +153,7 @@
 def choose(hots, values, parts, devices):
     levels = hots.shape[0] // (7 * devices)
     width = values.shape[1]
-    level_of, kind = kind_of(iota((1, width), 1), parts)
+    level_of, kind = kind_of(iota((1, width), 1) % (128 if parts == 1 else 256), parts)
     total = jnp.zeros((devices, width), F32)
     for level in range(levels):
         at = level * 7 * devices
@@ -167,20 +176,7 @@
     return pl.ds(pl.multiple_of(device * 8, 8), 8)
 
 
-def block_copy(source, target, send, recv, devices, me, step):
-    peer = lax.rem(me + step, devices)
-    return pltpu.make_async_remote_copy(
-        src_ref=source.at[block_rows(peer)],
-        dst_ref=target.at[block_rows(me)],
-        send_sem=send,
-        recv_sem=recv,
-        device_id=(peer,),
-        device_id_type=MESH,
-    )
-
-
-def back_copy(source, target, send, recv, devices, me, step):
-    peer = lax.rem(me + devices - step, devices)
+def block_copy(source, target, send, recv, peer, me):
     return pltpu.make_async_remote_copy(
         src_ref=source.at[block_rows(peer)],
         dst_ref=target.at[block_rows(me)],
@@ -258,46 +254,48 @@
     return start, forward, finish
 
 
-def hat(coord, rows, start):
-    ids = iota((rows, coord.shape[1]), 0).astype(F32) + start
+def hat(coord, rows):
+    ids = iota((rows, coord.shape[1]), 0).astype(F32)
     return jnp.maximum(0.0, 1.0 - jnp.abs(coord - ids))
 
 
-def group_sources(devices, me, block):
-    return [lax.rem(me + devices - (block * SOURCES + 1 + part), devices) for part in range(SOURCES)]
-
-
-def group_fields(inbox, sources):
-    fields = []
-    for field in range(4):
-        rows = []
-        for source in sources:
-            for order in range(2):
-                rows.append(inbox[pl.ds(source * 8 + (order * 4 + field), 1), :])
-        fields.append(jnp.concatenate(rows, axis=1))
-    return fields
-
-
-def fill_deposit(fields, short, weighted):
-    mass, x, y, z = fields
+def group_fields(inbox, first):
+    return [inbox[pl.ds(first + field, GROUP, stride=4), :] for field in range(4)]
+
+
+def flat(ref, first, stride):
+    return jnp.concatenate([ref[pl.ds(first + t * stride, 1), :] for t in range(GROUP)], axis=1)
+
+
+def end_hat(coord):
+    return jnp.maximum(0.0, 1.0 - jnp.abs(coord - float(SIDE)))
+
+
+def keep(rows, values):
+    for place, value in enumerate(values):
+        rows[place * GROUP : (place + 1) * GROUP, :] = value
+    return [flat(rows, place * GROUP, 1) for place in range(len(values))]
+
+
+def fill_deposit(inbox, first, rows, short, weighted):
+    mass, x, y, z = group_fields(inbox, first)
     chunk = jnp.where(y >= 2.0 * CHUNK, 2.0, jnp.where(y >= CHUNK, 1.0, 0.0))
-    hat_y = hat(y - chunk * CHUNK, 16, 0.0)
-    hat_z = hat(z, SIDE, 0.0)
+    row_of = 2.0 * chunk + jnp.where(mass < 0.0, 1.0, 0.0)
+    size = jnp.abs(mass)
+    owns = [jnp.where(row_of == float(place), size, 0.0) for place in range(CHUNKS * 2)]
+    rest = [y - chunk * CHUNK, end_hat(z), row_of, size * end_hat(x)]
+    *owns, near_y, end_z, row_of, end_x = keep(rows, owns + rest)
+    hat_x = hat(flat(inbox, first + 1, 4), SIDE)
+    hat_y = hat(near_y, 16)
+    hat_z = hat(flat(inbox, first + 3, 4), SIDE)
     for row in range(CHUNK + 1):
         short[row * SIDE : (row + 1) * SIDE, :] = (hat_y[row : row + 1, :] * hat_z).astype(BF16)
-    tops = jnp.where(iota((16, LANES), 0) <= CHUNK, hat_y * hat(z, 1, float(SIDE)), 0.0)
-    short[SHORT : SHORT + 16, :] = tops.astype(BF16)
-    hat_x = hat(x, SIDE, 0.0)
-    for place in range(CHUNKS):
-        for level in range(2):
-            own = jnp.maximum(mass if level == 0 else -mass, 0.0)
-            own = jnp.where(chunk == float(place), own, 0.0)
-            at = (place * 2 + level) * SIDE
-            weighted[at : at + SIDE, :] = (own * hat_x).astype(BF16)
-    row_of = 2.0 * chunk + jnp.where(mass < 0.0, 1.0, 0.0)
-    ends = jnp.where(iota((16, LANES), 0).astype(F32) == row_of, jnp.abs(mass), 0.0)
+    short[SHORT : SHORT + 16, :] = (hat_y * end_z).astype(BF16)
+    for place, own in enumerate(owns):
+        weighted[place * SIDE : (place + 1) * SIDE, :] = (own * hat_x).astype(BF16)
+    ends = jnp.where(iota((16, LANES), 0).astype(F32) == row_of, end_x, 0.0)
     at = CHUNKS * 2 * SIDE
-    weighted[at : at + 16, :] = (ends * hat(x, 1, float(SIDE))).astype(BF16)
+    weighted[at : at + 16, :] = ends.astype(BF16)
 
 
 def add_deposit(short, weighted, total):
@@ -307,37 +305,38 @@
     total[:, 0 : product.shape[1]] += product
 
 
-def fill_cross(fields, cross):
-    _, _, y, z = fields
-    hat_y, hat_z = hat(y, SIDE, 0.0), hat(z, SIDE, 0.0)
-    end_y, end_z = hat(y, 1, float(SIDE)), hat(z, 1, float(SIDE))
+def fill_cross(inbox, first, rows, cross):
+    _, _, y, z = group_fields(inbox, first)
+    end_y, end_z = end_hat(y), end_hat(z)
+    end_y, end_z, end_both = keep(rows, [end_y, end_z, end_y * end_z])
+    hat_y = hat(flat(inbox, first + 2, 4), SIDE)
+    hat_z = hat(flat(inbox, first + 3, 4), SIDE)
     for row in range(SIDE):
         cross[row * SIDE : (row + 1) * SIDE, :] = (hat_y[row : row + 1, :] * hat_z).astype(BF16)
     cross[CELLS : CELLS + 32, :] = (end_y * hat_z).astype(BF16)
     cross[CELLS + 32 : CELLS + 64, :] = (hat_y * end_z).astype(BF16)
-    last = jnp.where(iota((16, LANES), 0) == 0, end_y * end_z, 0.0)
+    last = jnp.where(iota((16, LANES), 0) == 0, end_both, 0.0)
     cross[CELLS + 64 : CELLS + 80, :] = last.astype(BF16)
 
 
-def sample(fields, sources, table, cross, kicks):
-    mass, x, _, _ = fields
-    rows = table.shape[0] - 16
-    depth = rows // 2
+def sample(inbox, first, rows, table, cross, kicks):
+    mass, x, _, _ = group_fields(inbox, first)
+    (end_x,) = keep(rows, [end_hat(x)])
+    hat_x = hat(flat(inbox, first + 1, 4), SIDE)
+    upper_level = flat(inbox, first, 4) < 0.0
+    amount = table.shape[0] - 16
+    depth = amount // 2
     sampled = jnp.dot(table[...], cross[...], preferred_element_type=F32)
-    hat_x, end_x = hat(x, SIDE, 0.0), hat(x, 1, float(SIDE))
-    upper_level = mass < 0.0
     for axis in range(3):
         at = axis * SIDE
         picked = jnp.where(
             upper_level, sampled[depth + at : depth + at + SIDE, :], sampled[at : at + SIDE, :]
         )
-        at = rows + axis
+        at = amount + axis
         far = jnp.where(upper_level, sampled[at + 3 : at + 4, :], sampled[at : at + 1, :])
         value = jnp.sum(hat_x * picked, axis=0, keepdims=True) + end_x * far
-        for part, source in enumerate(sources):
-            for order in range(2):
-                lanes = slice((part * 2 + order) * 128, (part * 2 + order + 1) * 128)
-                kicks[pl.ds(source * 8 + (order * 4 + axis), 1), :] = value[:, lanes]
+        for t in range(GROUP):
+            kicks[pl.ds(first + (t * 4 + axis), 1), :] = value[:, t * 128 : (t + 1) * 128]
 
 
 def spread_deposit(total, wide):
@@ -394,6 +393,11 @@
     short_b,
     weighted_a,
     weighted_b,
+    rows_a,
+    rows_b,
+    rows_c,
+    rows_d,
+    picks_back,
     total,
     wide,
     own_sem,
@@ -407,7 +411,8 @@
     me = lax.axis_index("boxes")
     depth = 3 * SIDE
     rows = levels * depth
-    groups = devices // SOURCES
+    groups = devices // INNER
+    my_row = me // INNER
     pairs = groups // 2
 
     loads = [
@@ -440,32 +445,11 @@
     fields = [jnp.where(level_ref[...] == 0, mass_ref[...], -mass_ref[...])]
     for axis in range(3):
         fields.append(digits[axis].astype(F32) + frac_ref[axis])
-    packed = jnp.dot(
-        picks, jnp.concatenate(fields, axis=1), preferred_element_type=F32, precision=HIGHEST
-    )
+    packed = exact_dot(picks, jnp.concatenate(fields, axis=1))
     for order in range(2):
         for field in range(4):
             part = packed[order * devices : (order + 1) * devices, field * 128 : field * 128 + 128]
             outbox[pl.ds(order * 4 + field, devices, stride=8), :] = part
-
-    pl.semaphore_wait(barrier, devices - 1)
-
-    force_hops = [
-        rim_hops(force_out, force_middle.at[0], force_spread, rim_sems.at[0], devices, me),
-        rim_hops(force_next, force_middle.at[1], force_last, rim_sems.at[1], devices, me),
-    ]
-    mass_hops = [
-        rim_hops(mass_out, mass_middle.at[0], mass_spread, rim_sems.at[2], devices, me),
-        rim_hops(mass_next, mass_middle.at[1], mass_last, rim_sems.at[3], devices, me),
-    ]
-
-    def tile_copy(step):
-        group = (step - 1) // SOURCES
-        return block_copy(outbox, inbox, tile_send, tile_recv.at[group], devices, me, step)
-
-    each(devices, lambda step: tile_copy(step).start())
-    own = pltpu.make_async_copy(outbox.at[block_rows(me)], inbox.at[block_rows(me)], own_sem)
-    own.start()
 
     loads[4].wait()
     force = force_ref[...]
@@ -480,12 +464,40 @@
     for half in range(2):
         block = jnp.transpose(values[half * 128 : half * 128 + 128, :])
         force_out[:, :, half, :] = block.reshape(devices // INNER, INNER, 128)
+    pl.semaphore_wait(barrier, devices - 1)
+
+    force_hops = [
+        rim_hops(force_out, force_middle.at[0], force_spread, rim_sems.at[0], devices, me),
+        rim_hops(force_next, force_middle.at[1], force_last, rim_sems.at[1], devices, me),
+    ]
+    mass_hops = [
+        rim_hops(mass_out, mass_middle.at[0], mass_spread, rim_sems.at[2], devices, me),
+        rim_hops(mass_next, mass_middle.at[1], mass_last, rim_sems.at[3], devices, me),
+    ]
+
+    def tile_copy(hop, peer):
+        return block_copy(outbox, inbox, tile_send, tile_recv.at[hop], peer, me)
+
+    def send_tiles(hop):
+        target = lax.rem(my_row + hop, groups) * INNER
+        each(INNER, lambda step: tile_copy(hop, target + lax.rem(me + step, INNER)).start())
+
+        @pl.when(hop > 0)
+        def _():
+            tile_copy(hop, target + lax.rem(me, INNER)).start()
+
     force_hops[0][0]()
+    send_tiles(0)
+    each(groups, send_tiles)
+    own = pltpu.make_async_copy(outbox.at[block_rows(me)], inbox.at[block_rows(me)], own_sem)
+    own.start()
+    force_hops[0][1]()
 
     for level in range(levels):
         ways = rim_sources(box_owner, level, devices)
         for way in range(2):
             hots[pl.ds((way * levels + level) * 7 * devices, 7 * devices), :] = ways[way]
+    picks_back[...] = slot_picks(owner_ref, count_ref[0], False)
     table[0:rows, 0:CELLS] = force
     blank = jnp.zeros((WIDE - CELLS - 80, LANES), BF16)
     cross_a[CELLS + 80 : WIDE, :] = blank
@@ -510,7 +522,8 @@
         high = values.astype(BF16)
         rest = (values - high.astype(F32)).astype(BF16)
         way = hots[levels * 7 * devices : 2 * levels * 7 * devices, :]
-        chosen = choose(way, high, 1, devices) + choose(way, rest, 1, devices)
+        chosen = choose(way, jnp.concatenate([high, rest], axis=1), 1, devices)
+        chosen = chosen[:, 0:128] + chosen[:, 128:256]
         mass_next[:, :, 0, :] = chosen.reshape(devices // INNER, INNER, 128)
         mass_hops[1][0]()
 
@@ -518,39 +531,45 @@
         for place, act in zip(at, acts):
             pl.when(pair == place)(act)
 
-    def await_group(block, last):
-        if last:
+    def await_group(hop):
+        amount = devices // groups * 8
+        if isinstance(hop, int) and hop == 0:
             own.wait()
-        amount = (SOURCES - 1 if last else SOURCES) * 8
+            amount -= 8
         pltpu.make_async_remote_copy(
             src_ref=outbox.at[pl.ds(0, amount)],
             dst_ref=inbox.at[pl.ds(0, amount)],
             send_sem=tile_send,
-            recv_sem=tile_recv.at[block],
+            recv_sem=tile_recv.at[hop],
             device_id=(lax.rem(me + 1, devices),),
             device_id_type=MESH,
         ).wait_recv()
 
-    def fill(block, short, weighted):
-        sources = group_sources(devices, me, block)
-        fill_deposit(group_fields(inbox, sources), short, weighted)
-
-    await_group(0, False)
-    fill(0, short_a, weighted_a)
+    def first_of(hop):
+        return pl.multiple_of(lax.rem(my_row + groups - hop, groups) * (INNER * 8), 8)
+
+    def fill_a(hop):
+        fill_deposit(inbox, first_of(hop), rows_a, short_a, weighted_a)
+
+    def fill_b(hop):
+        fill_deposit(inbox, first_of(hop), rows_b, short_b, weighted_b)
+
+    await_group(0)
+    fill_a(0)
 
     def deposit_pair(pair, carry):
-        stages(pair, FORCE_STAGES, (force_hops[0][1], force_relay, force_hops[1][1]))
-        await_group(2 * pair + 1, False)
-        await_group(2 * pair + 2, False)
-        fill(2 * pair + 1, short_b, weighted_b)
+        stages(pair, FORCE_STAGES, (force_relay, force_hops[1][1]))
+        await_group(2 * pair + 1)
+        await_group(2 * pair + 2)
+        fill_b(2 * pair + 1)
         add_deposit(short_a, weighted_a, total)
-        fill(2 * pair + 2, short_a, weighted_a)
+        fill_a(2 * pair + 2)
         add_deposit(short_b, weighted_b, total)
         return carry
 
     lax.fori_loop(0, pairs - 1, deposit_pair, 0)
-    await_group(groups - 1, True)
-    fill(groups - 1, short_b, weighted_b)
+    await_group(groups - 1)
+    fill_b(groups - 1)
     add_deposit(short_a, weighted_a, total)
     add_deposit(short_b, weighted_b, total)
 
@@ -576,42 +595,47 @@
     fronts.append(jnp.zeros((16 - len(fronts), WIDE), F32))
     table[rows : rows + 16, :] = jnp.concatenate(fronts, axis=0).astype(BF16)
 
-    def kick_copy(step):
-        return back_copy(kicks, returned, kick_send, kick_recv, devices, me, step)
-
-    def cross_of(block, cross):
-        fill_cross(group_fields(inbox, group_sources(devices, me, block)), cross)
-
-    def sample_of(block, cross):
-        sources = group_sources(devices, me, block)
-        sample(group_fields(inbox, sources), sources, table, cross, kicks)
-
-    def send_group(block, last):
-        for part in range(SOURCES - 1 if last else SOURCES):
-            kick_copy(block * SOURCES + 1 + part).start()
-
-    cross_of(0, cross_a)
+    def kick_copy(peer):
+        return block_copy(kicks, returned, kick_send, kick_recv, peer, me)
+
+    def send_kicks(hop):
+        target = lax.rem(my_row + groups - hop, groups) * INNER
+        for place in range(INNER):
+            kick_copy(target + place).start()
+
+    def cross_a_of(hop):
+        fill_cross(inbox, first_of(hop), rows_a, cross_a)
+
+    def cross_b_of(hop):
+        fill_cross(inbox, first_of(hop), rows_b, cross_b)
+
+    def sample_a_of(hop):
+        sample(inbox, first_of(hop), rows_c, table, cross_a, kicks)
+
+    def sample_b_of(hop):
+        sample(inbox, first_of(hop), rows_d, table, cross_b, kicks)
+
+    cross_a_of(1)
 
     def sample_pair(pair, carry):
         stages(pair, MASS_STAGES, (mass_hops[0][1], mass_relay, mass_hops[1][1]))
-        cross_of(2 * pair + 1, cross_b)
-        sample_of(2 * pair, cross_a)
-        cross_of(2 * pair + 2, cross_a)
-        sample_of(2 * pair + 1, cross_b)
-        send_group(2 * pair, False)
-        send_group(2 * pair + 1, False)
+        cross_b_of(2 * pair + 2)
+        sample_a_of(2 * pair + 1)
+        cross_a_of(2 * pair + 3)
+        sample_b_of(2 * pair + 2)
+        send_kicks(2 * pair + 1)
+        send_kicks(2 * pair + 2)
         return carry
 
     lax.fori_loop(0, pairs - 1, sample_pair, 0)
-    cross_of(groups - 1, cross_b)
-    sample_of(groups - 2, cross_a)
-    sample_of(groups - 1, cross_b)
-    send_group(groups - 2, False)
-    send_group(groups - 1, True)
+    cross_b_of(0)
+    sample_a_of(groups - 1)
+    send_kicks(groups - 1)
+    sample_b_of(0)
+    each(INNER, lambda step: kick_copy(my_row * INNER + lax.rem(me + step, INNER)).start())
     kept = pltpu.make_async_copy(kicks.at[block_rows(me)], returned.at[block_rows(me)], own_sem)
     kept.start()
 
-    picks = slot_picks(owner_ref, count_ref[0], False)
     mass_hops[1][2]()
     values = jnp.transpose(mass_last[:, :, 0, :].reshape(devices, 128))
     edges, fronts = unpack_rims(values, levels)
@@ -621,12 +645,11 @@
         + jnp.where(first_row, fronts[level][:, CELLS:WIDE], 0.0)
         for level in range(levels)
     ]
-    added = jnp.dot(
-        jnp.concatenate(low, axis=0),
-        plane_pick(F32, True),
-        preferred_element_type=F32,
-        precision=HIGHEST,
-    )
+    low = jnp.concatenate(low, axis=0)
+    high = low.astype(BF16)
+    pair = jnp.concatenate([high, (low - high.astype(F32)).astype(BF16)], axis=0)
+    added = jnp.dot(pair, plane_pick(BF16, True), preferred_element_type=F32)
+    added = added[0 : levels * SIDE, :] + added[levels * SIDE : 2 * levels * SIDE, :]
     for level in range(levels):
         at = slice(level * SIDE, (level + 1) * SIDE)
         density[at, :] += added[at, :] + jnp.where(first_row, fronts[level][:, 0:CELLS], 0.0)
@@ -638,9 +661,7 @@
     for order in range(2):
         columns = [returned[pl.ds(order * 4 + axis, devices, stride=8), :] for axis in range(3)]
         parts.append(jnp.concatenate(columns, axis=1))
-    mine = jnp.dot(
-        picks, jnp.concatenate(parts, axis=0), preferred_element_type=F32, precision=HIGHEST
-    )
+    mine = exact_dot(picks_back[...], jnp.concatenate(parts, axis=0))
     for axis in range(3):
         kick[axis] = mine[:, axis * 128 : (axis + 1) * 128]
 
@@ -689,11 +710,16 @@
             pltpu.VMEM((SHORT + 16, LANES), BF16),
             pltpu.VMEM((spread_rows, LANES), BF16),
             pltpu.VMEM((spread_rows, LANES), BF16),
+            pltpu.VMEM((10 * GROUP, 128), F32),
+            pltpu.VMEM((10 * GROUP, 128), F32),
+            pltpu.VMEM((GROUP, 128), F32),
+            pltpu.VMEM((GROUP, 128), F32),
+            pltpu.VMEM((tiles, 2 * devices), BF16),
             pltpu.VMEM((SHORT + 16, 256), F32),
             pltpu.VMEM((WIDE, 128), F32),
             dma,
             dma,
-            dma((devices // SOURCES,)),
+            dma((devices // INNER,)),
             dma,
             dma,
             dma((5,)),

time: 70.8 us -> 68.8 us (0.972)
  Pallas kernels: 67 us -> 64.9 us
    pallas_call x1, Pallas kernels: 67 us -> 64.9 us  [on_device(): pl.pallas_call(functools.partial(kernel, devices, levels), out_shape=(sha...]
where the time goes in v3:
time: 68.8 us; the launch traced here: 68.6 us
  Pallas kernels  64.9 us (94%)
  local copies, waits for them, and re-layouts  2.39 us (3%)
  between operations  1.3 us (2%)
    pallas_call x1, Pallas kernels, on_device(): pl.pallas_call(functools.partial(kernel, devices, levels), out_shape=(sha...  64.9 us
    unnamed x4, local copies, waits for them, and re-layouts  2.39 us

profile of v3, /device:TPU:1, one launch (start us, length us, event | category | flops | bytes accessed | tf_op | source)
XLA Modules:
  0.0 68.6 jit_solution(8266714276651483073)
XLA Ops:
  1.3 64.9 %deposit_and_sample.1 = (f32[64,1024]{1,0:T(8,128)}, f32[3,128,128]{2,1,0:T(8,128)}) custom-call(s32[1]{0:T(128)S(6)} %copy.12.count_ref, s32[1,128]{1,0:T(1,128)} %bitcast.9, s32[2,128]{1,0:T(2,128)} %box_owner.1, f32[128,128]{1,0:T(8,128)} %mass_in.1, f32[3,128,128]{2,1,0:T(8,128)} %bitcast.8, s32[128,128]{1,0:T(8,128)} %cell_in.1, s32[128,128]{1,0:T(8,128)} %level_in.1, ...), custom_call_target="tpu_custom_call" | custom-call | tf_op jit(solution)/shard_map/deposit_and_sample/pallas_call | solution.py:682
  66.2 0.0 copy-start
  66.2 1.7 %copy.13 = f32[2,32,1024]{2,1,0:T(8,128)} copy(f32[2,32,1024]{2,1,0:T(8,128)} %bitcast.6) | data formatting | bytes 524288
  67.9 0.0 copy-done
  67.9 0.7 copy.14
Async XLA Ops:
  66.2 1.7 %copy-start = (f32[3,128,128]{2,1,0:T(8,128)S(1)}, f32[3,128,128]{2,1,0:T(8,128)}, u32[]{:S(2)}) copy-start(f32[3,128,128]{2,1,0:T(8,128)} %get-tuple-element.5) | copy-start | bytes 589828

commit v4 on v3

--- a/solution.py
+++ b/solution.py
@@ -22,7 +22,7 @@
 CHUNK = 11
 CHUNKS = 3
 SHORT = (CHUNK + 1) * SIDE
-FORCE_STAGES = (4, 6)
+FORCE_STAGE = 5
 MASS_STAGES = (1, 3, 5)
 
 direction_table = np.array(
@@ -254,6 +254,28 @@
     return start, forward, finish
 
 
+def rim_copy(source, target, sems, peer, me):
+    return pltpu.make_async_remote_copy(
+        src_ref=source.at[peer],
+        dst_ref=target.at[me],
+        send_sem=sems.at[0],
+        recv_sem=sems.at[1],
+        device_id=(peer,),
+        device_id_type=MESH,
+    )
+
+
+def all_rims(source, target, sems, devices, me):
+    return pltpu.make_async_remote_copy(
+        src_ref=source.at[pl.ds(0, devices - 1)],
+        dst_ref=target.at[pl.ds(0, devices - 1)],
+        send_sem=sems.at[0],
+        recv_sem=sems.at[1],
+        device_id=(lax.rem(me + 1, devices),),
+        device_id_type=MESH,
+    )
+
+
 def hat(coord, rows):
     ids = iota((rows, coord.shape[1]), 0).astype(F32)
     return jnp.maximum(0.0, 1.0 - jnp.abs(coord - ids))
@@ -357,8 +379,8 @@
     devices,
     levels,
     count_ref,
-    owner_ref,
-    box_owner,
+    owner_in,
+    box_in,
     mass_in,
     frac_in,
     cell_in,
@@ -370,6 +392,8 @@
     inbox,
     kicks,
     returned,
+    owner_ref,
+    box_owner,
     mass_ref,
     frac_ref,
     cell_ref,
@@ -419,11 +443,13 @@
         pltpu.make_async_copy(source, target, load_sem.at[place])
         for place, (source, target) in enumerate(
             [
+                (owner_in, owner_ref),
                 (mass_in, mass_ref),
                 (frac_in, frac_ref),
                 (cell_in, cell_ref),
                 (level_in, level_ref),
                 (force_in, force_ref),
+                (box_in, box_owner),
             ]
         )
     ]
@@ -437,8 +463,9 @@
         ),
     )
 
+    loads[0].wait()
     picks = slot_picks(owner_ref, count_ref[0], True)
-    for load in loads[:4]:
+    for load in loads[1:5]:
         load.wait()
     cell = cell_ref[...]
     digits = [cell // CELLS, cell // SIDE % SIDE, cell % SIDE]
@@ -451,7 +478,8 @@
             part = packed[order * devices : (order + 1) * devices, field * 128 : field * 128 + 128]
             outbox[pl.ds(order * 4 + field, devices, stride=8), :] = part
 
-    loads[4].wait()
+    loads[5].wait()
+    loads[6].wait()
     force = force_ref[...]
     edges = jnp.dot(force, plane_pick(BF16, False), preferred_element_type=F32)
     fronts = []
@@ -466,10 +494,7 @@
         force_out[:, :, half, :] = block.reshape(devices // INNER, INNER, 128)
     pl.semaphore_wait(barrier, devices - 1)
 
-    force_hops = [
-        rim_hops(force_out, force_middle.at[0], force_spread, rim_sems.at[0], devices, me),
-        rim_hops(force_next, force_middle.at[1], force_last, rim_sems.at[1], devices, me),
-    ]
+    force_hops = rim_hops(force_out, force_middle, force_spread, rim_sems.at[0], devices, me)
     mass_hops = [
         rim_hops(mass_out, mass_middle.at[0], mass_spread, rim_sems.at[2], devices, me),
         rim_hops(mass_next, mass_middle.at[1], mass_last, rim_sems.at[3], devices, me),
@@ -486,12 +511,12 @@
         def _():
             tile_copy(hop, target + lax.rem(me, INNER)).start()
 
-    force_hops[0][0]()
+    force_hops[0]()
     send_tiles(0)
     each(groups, send_tiles)
     own = pltpu.make_async_copy(outbox.at[block_rows(me)], inbox.at[block_rows(me)], own_sem)
     own.start()
-    force_hops[0][1]()
+    force_hops[1]()
 
     for level in range(levels):
         ways = rim_sources(box_owner, level, devices)
@@ -506,15 +531,20 @@
     kicks[...] = jnp.zeros_like(kicks)
 
     def force_relay():
-        force_hops[0][2]()
+        force_hops[2]()
         values = jnp.concatenate(
             [force_spread[:, :, half, :].reshape(devices, 128) for half in range(2)], axis=1
         )
         chosen = choose(hots[0 : levels * 7 * devices, :], values.astype(BF16), 3, devices)
         for half in range(2):
-            block = chosen[:, half * 128 : half * 128 + 128]
-            force_next[:, :, half, :] = block.reshape(devices // INNER, INNER, 128)
-        force_hops[1][0]()
+            force_next[:, half, :] = chosen[:, half * 128 : half * 128 + 128]
+        each(
+            devices,
+            lambda step: rim_copy(
+                force_next, force_last, rim_sems.at[1], lax.rem(me + step, devices), me
+            ).start(),
+        )
+        force_last[me] = force_next[me]
 
     def mass_relay():
         mass_hops[0][2]()
@@ -558,7 +588,7 @@
     fill_a(0)
 
     def deposit_pair(pair, carry):
-        stages(pair, FORCE_STAGES, (force_relay, force_hops[1][1]))
+        pl.when(pair == FORCE_STAGE)(force_relay)
         await_group(2 * pair + 1)
         await_group(2 * pair + 2)
         fill_b(2 * pair + 1)
@@ -585,37 +615,36 @@
     mass_out[:, :, 0, :] = jnp.transpose(values).reshape(devices // INNER, INNER, 128)
     mass_hops[0][0]()
 
-    force_hops[1][2]()
+    def kick_copy(peer):
+        return block_copy(kicks, returned, kick_send, kick_recv, peer, me)
+
+    def send_kicks(hop):
+        target = lax.rem(my_row + groups - hop, groups) * INNER
+        for place in range(INNER):
+            kick_copy(target + place).start()
+
+    def cross_a_of(hop):
+        fill_cross(inbox, first_of(hop), rows_a, cross_a)
+
+    def cross_b_of(hop):
+        fill_cross(inbox, first_of(hop), rows_b, cross_b)
+
+    def sample_a_of(hop):
+        sample(inbox, first_of(hop), rows_c, table, cross_a, kicks)
+
+    def sample_b_of(hop):
+        sample(inbox, first_of(hop), rows_d, table, cross_b, kicks)
+
+    cross_a_of(1)
+
+    all_rims(force_next, force_last, rim_sems.at[1], devices, me).wait()
     values = jnp.concatenate(
-        [jnp.transpose(force_last[:, :, half, :].reshape(devices, 128)) for half in range(2)],
-        axis=0,
+        [jnp.transpose(force_last[:, half, :]) for half in range(2)], axis=0
     )
     edges, fronts = unpack_rims(values, levels * 3)
     table[0:rows, CELLS:WIDE] = edges.astype(BF16)
     fronts.append(jnp.zeros((16 - len(fronts), WIDE), F32))
     table[rows : rows + 16, :] = jnp.concatenate(fronts, axis=0).astype(BF16)
-
-    def kick_copy(peer):
-        return block_copy(kicks, returned, kick_send, kick_recv, peer, me)
-
-    def send_kicks(hop):
-        target = lax.rem(my_row + groups - hop, groups) * INNER
-        for place in range(INNER):
-            kick_copy(target + place).start()
-
-    def cross_a_of(hop):
-        fill_cross(inbox, first_of(hop), rows_a, cross_a)
-
-    def cross_b_of(hop):
-        fill_cross(inbox, first_of(hop), rows_b, cross_b)
-
-    def sample_a_of(hop):
-        sample(inbox, first_of(hop), rows_c, table, cross_a, kicks)
-
-    def sample_b_of(hop):
-        sample(inbox, first_of(hop), rows_d, table, cross_b, kicks)
-
-    cross_a_of(1)
 
     def sample_pair(pair, carry):
         stages(pair, MASS_STAGES, (mass_hops[0][1], mass_relay, mass_hops[1][1]))
@@ -682,13 +711,15 @@
     density, kick = pl.pallas_call(
         functools.partial(kernel, devices, levels),
         out_shape=(shape((levels * SIDE, CELLS), F32), shape((3, tiles, width), F32)),
-        in_specs=[smem, vmem, vmem] + [pl.BlockSpec(memory_space=pl.ANY)] * 5,
+        in_specs=[smem] + [pl.BlockSpec(memory_space=pl.ANY)] * 7,
         out_specs=(vmem, vmem),
         scratch_shapes=[
             blocks,
             blocks,
             blocks,
             blocks,
+            pltpu.VMEM((1, tiles), jnp.int32),
+            pltpu.VMEM(box_owner.shape, jnp.int32),
             pltpu.VMEM((tiles, width), F32),
             pltpu.VMEM((3, tiles, width), F32),
             pltpu.VMEM((tiles, width), jnp.int32),
@@ -696,10 +727,11 @@
             pltpu.VMEM((rows, CELLS), BF16),
             pltpu.VMEM((2 * levels * 7 * devices, devices), BF16),
         ]
-        + [pltpu.VMEM((devices // INNER, INNER, 2, 128), F32)] * 4
+        + [pltpu.VMEM((devices // INNER, INNER, 2, 128), F32)] * 2
+        + [pltpu.VMEM((devices, 2, 128), F32)] * 2
         + [pltpu.VMEM((devices // INNER, INNER, 1, 128), F32)] * 4
         + [
-            pltpu.VMEM((2, INNER, devices // INNER, 2, 128), F32),
+            pltpu.VMEM((INNER, devices // INNER, 2, 128), F32),
             pltpu.VMEM((2, INNER, devices // INNER, 1, 128), F32),
         ]
         + [
@@ -722,7 +754,7 @@
             dma((devices // INNER,)),
             dma,
             dma,
-            dma((5,)),
+            dma((7,)),
             dma((4, 4)),
         ],
         compiler_params=pltpu.CompilerParams(

time: 68.8 us -> 65.9 us (0.958)
  Pallas kernels: 64.9 us -> 62.1 us
    pallas_call x1, Pallas kernels: 64.9 us -> 62.1 us  [on_device(): pl.pallas_call(functools.partial(kernel, devices, levels), out_shape=(sha...]
where the time goes in v4:
time: 65.9 us; the launch traced here: 65.8 us
  Pallas kernels  62.1 us (94%)
  local copies, waits for them, and re-layouts  2.39 us (4%)
  between operations  1.3 us (2%)
    pallas_call x1, Pallas kernels, on_device(): pl.pallas_call(functools.partial(kernel, devices, levels), out_shape=(sha...  62.1 us
    unnamed x4, local copies, waits for them, and re-layouts  2.39 us

profile of v4, /device:TPU:1, one launch (start us, length us, event | category | flops | bytes accessed | tf_op | source)
XLA Modules:
  0.0 65.8 jit_solution(13429132732473201617)
XLA Ops:
  1.3 62.1 %deposit_and_sample.1 = (f32[64,1024]{1,0:T(8,128)}, f32[3,128,128]{2,1,0:T(8,128)}) custom-call(s32[1]{0:T(128)S(6)} %copy.12.count_ref, s32[1,128]{1,0:T(1,128)} %bitcast.9, s32[2,128]{1,0:T(2,128)} %box_in.1, f32[128,128]{1,0:T(8,128)} %mass_in.1, f32[3,128,128]{2,1,0:T(8,128)} %bitcast.8, s32[128,128]{1,0:T(8,128)} %cell_in.1, s32[128,128]{1,0:T(8,128)} %level_in.1, ...), custom_call_target="tpu_custom_call" | custom-call | tf_op jit(solution)/shard_map/deposit_and_sample/pallas_call | solution.py:711
  63.4 0.0 copy-start
  63.4 1.7 %copy.13 = f32[2,32,1024]{2,1,0:T(8,128)} copy(f32[2,32,1024]{2,1,0:T(8,128)} %bitcast.6) | data formatting | bytes 524288
  65.1 0.0 copy-done
  65.1 0.7 %copy.14 = f32[128,3,128]{2,0,1:T(8,128)} copy(f32[128,3,128]{2,0,1:T(8,128)S(1)} %bitcast.7) | data formatting | bytes 393216
Async XLA Ops:
  63.4 1.7 %copy-start = (f32[3,128,128]{2,1,0:T(8,128)S(1)}, f32[3,128,128]{2,1,0:T(8,128)}, u32[]{:S(2)}) copy-start(f32[3,128,128]{2,1,0:T(8,128)} %get-tuple-element.5) | copy-start | bytes 589828

commit v5 on v4

--- a/solution.py
+++ b/solution.py
@@ -126,7 +126,7 @@
     return jnp.concatenate(picks, axis=0 if by_slot else 1).astype(BF16)
 
 
-def rim_sources(box_owner, level, devices):
+def rim_sources(box_owner, level, devices, sign):
     lat_y = devices // (LAT_X * LAT_Z)
     square = (devices, devices)
     across = jnp.broadcast_to(box_owner[level : level + 1, :], square)
@@ -135,19 +135,16 @@
     places = iota(square, 0).astype(F32).astype(BF16)
     box = jnp.dot(hot, places, preferred_element_type=F32).astype(jnp.int32)
     at = [box // (lat_y * LAT_Z), box // LAT_Z % lat_y, box % LAT_Z]
-    found = []
-    for sign in (1, -1):
-        hots = []
-        for step in direction_table:
-            near = [
-                (at[axis] + (sign * int(step[axis]) + extent)) % extent
-                for axis, extent in enumerate((LAT_X, lat_y, LAT_Z))
-            ]
-            wanted = (near[0] * lat_y + near[1]) * LAT_Z + near[2]
-            hots.append(ones_at(wanted == iota(square, 1), BF16))
-        owners = jnp.dot(jnp.concatenate(hots, axis=0), down, preferred_element_type=F32)
-        found.append(ones_at(owners == iota(owners.shape, 1).astype(F32), BF16))
-    return found
+    hots = []
+    for step in direction_table:
+        near = [
+            (at[axis] + (sign * int(step[axis]) + extent)) % extent
+            for axis, extent in enumerate((LAT_X, lat_y, LAT_Z))
+        ]
+        wanted = (near[0] * lat_y + near[1]) * LAT_Z + near[2]
+        hots.append(ones_at(wanted == iota(square, 1), BF16))
+    owners = jnp.dot(jnp.concatenate(hots, axis=0), down, preferred_element_type=F32)
+    return ones_at(owners == iota(owners.shape, 1).astype(F32), BF16)
 
 
 def choose(hots, values, parts, devices):
@@ -518,11 +515,12 @@
     own.start()
     force_hops[1]()
 
-    for level in range(levels):
-        ways = rim_sources(box_owner, level, devices)
-        for way in range(2):
-            hots[pl.ds((way * levels + level) * 7 * devices, 7 * devices), :] = ways[way]
-    picks_back[...] = slot_picks(owner_ref, count_ref[0], False)
+    def find_sources(way, sign):
+        for level in range(levels):
+            first = (way * levels + level) * 7 * devices
+            hots[pl.ds(first, 7 * devices), :] = rim_sources(box_owner, level, devices, sign)
+
+    find_sources(0, 1)
     table[0:rows, 0:CELLS] = force
     blank = jnp.zeros((WIDE - CELLS - 80, LANES), BF16)
     cross_a[CELLS + 80 : WIDE, :] = blank
@@ -637,6 +635,8 @@
 
     cross_a_of(1)
 
+    find_sources(1, -1)
+    picks_back[...] = slot_picks(owner_ref, count_ref[0], False)
     all_rims(force_next, force_last, rim_sems.at[1], devices, me).wait()
     values = jnp.concatenate(
         [jnp.transpose(force_last[:, half, :]) for half in range(2)], axis=0

time: 65.9 us -> 66.4 us (level)
  no operation moved by 1% of the time
where the time goes in v5:
time: 66.4 us; the launch traced here: 66.2 us
  Pallas kernels  62.5 us (94%)
  local copies, waits for them, and re-layouts  2.39 us (4%)
  between operations  1.3 us (2%)
    pallas_call x1, Pallas kernels, on_device(): pl.pallas_call(functools.partial(kernel, devices, levels), out_shape=(sha...  62.5 us
    unnamed x4, local copies, waits for them, and re-layouts  2.39 us

profile of v5, /device:TPU:1, one launch (start us, length us, event | category | flops | bytes accessed | tf_op | source)
XLA Modules:
  0.0 66.2 jit_solution(15431679616799509868)
XLA Ops:
  1.3 62.5 %deposit_and_sample.1 = (f32[64,1024]{1,0:T(8,128)}, f32[3,128,128]{2,1,0:T(8,128)}) custom-call(s32[1]{0:T(128)S(6)} %copy.12.count_ref, s32[1,128]{1,0:T(1,128)} %bitcast.9, s32[2,128]{1,0:T(2,128)} %box_in.1, f32[128,128]{1,0:T(8,128)} %mass_in.1, f32[3,128,128]{2,1,0:T(8,128)} %bitcast.8, s32[128,128]{1,0:T(8,128)} %cell_in.1, s32[128,128]{1,0:T(8,128)} %level_in.1, ...), custom_call_target="tpu_custom_call" | custom-call | tf_op jit(solution)/shard_map/deposit_and_sample/pallas_call | solution.py:711
  63.8 0.0 copy-start
  63.8 1.7 %copy.13 = f32[2,32,1024]{2,1,0:T(8,128)} copy(f32[2,32,1024]{2,1,0:T(8,128)} %bitcast.6) | data formatting | bytes 524288
  65.5 0.0 copy-done
  65.5 0.7 %copy.14 = f32[128,3,128]{2,0,1:T(8,128)} copy(f32[128,3,128]{2,0,1:T(8,128)S(1)} %bitcast.7) | data formatting | bytes 393216
Async XLA Ops:
  63.8 1.7 %copy-start = (f32[3,128,128]{2,1,0:T(8,128)S(1)}, f32[3,128,128]{2,1,0:T(8,128)}, u32[]{:S(2)}) copy-start(f32[3,128,128]{2,1,0:T(8,128)} %get-tuple-element.5) | copy-start | bytes 589828
